TPU v7x, 32 devices: a whole 2x2x4 slice. The times are simulated.
32 devices in a mesh: head: 2 (over y), blk: 16 (over z, x, core).
Axes of the slice: x: 2, y: 2, z: 4, core: 2. Of those that a mesh axis runs over, the one named last changes fastest.
Arguments:
- tokens: bfloat16 [16384, 768], P(('blk', 'head')), may hold values from -6 to 6
- cotangent: bfloat16 [16384, 768], P(('blk', 'head')), may hold values from -6 to 6
- doc_lengths: int32 [8], replicated, may hold values from 1 to 15872, 16384 in all
- global_blocks: int32 [2], replicated, may hold values from 0 to 255
- random_blocks: int32 [12, 256, 3], P('head', 'blk'), may hold values from 0 to 255, as said below
- query_weight: bfloat16 [768, 768], P(('head', 'blk')), may hold values from -0.21875 to 0.21875
- query_bias: bfloat16 [768], P(('head', 'blk')), may hold values from -3 to 3
- key_weight: bfloat16 [768, 768], P(('head', 'blk')), may hold values from -0.21875 to 0.21875
- value_weight: bfloat16 [768, 768], P(('head', 'blk')), may hold values from -0.21875 to 0.21875
- value_bias: bfloat16 [768], P(('head', 'blk')), may hold values from -3 to 3
- output_weight: bfloat16 [768, 768], P(('head', 'blk')), may hold values from -6 to 6
- output_bias: bfloat16 [768], P(('head', 'blk')), may hold values from -3 to 3
- first_gain: bfloat16 [768], P(('head', 'blk')), may hold values from 0.5 to 1.5
- first_shift: bfloat16 [768], P(('head', 'blk')), may hold values from -3 to 3
- up_weight: bfloat16 [768, 3072], P(('head', 'blk')), may hold values from -0.21875 to 0.21875
- up_bias: bfloat16 [3072], P(('head', 'blk')), may hold values from -3 to 3
- down_weight: bfloat16 [3072, 768], P(('head', 'blk')), may hold values from -0.109375 to 0.109375
- down_bias: bfloat16 [768], P(('head', 'blk')), may hold values from -3 to 3
- second_gain: bfloat16 [768], P(('head', 'blk')), may hold values from 0.5 to 1.5
- second_shift: bfloat16 [768], P(('head', 'blk')), may hold values from -3 to 3
Outputs:
- out: bfloat16 [16384, 768], P(('blk', 'head'))
- tokens_grad: float32 [16384, 768], P(('blk', 'head'))
- query_weight_grad: float32 [768, 768], P(('head', 'blk'))
- query_bias_grad: float32 [768], P(('head', 'blk'))
- key_weight_grad: float32 [768, 768], P(('head', 'blk'))
- value_weight_grad: float32 [768, 768], P(('head', 'blk'))
- value_bias_grad: float32 [768], P(('head', 'blk'))
- output_weight_grad: float32 [768, 768], P(('head', 'blk'))
- output_bias_grad: float32 [768], P(('head', 'blk'))
- first_gain_grad: float32 [768], P(('head', 'blk'))
- first_shift_grad: float32 [768], P(('head', 'blk'))
- up_weight_grad: float32 [768, 3072], P(('head', 'blk'))
- up_bias_grad: float32 [3072], P(('head', 'blk'))
- down_weight_grad: float32 [3072, 768], P(('head', 'blk'))
- down_bias_grad: float32 [768], P(('head', 'blk'))
- second_gain_grad: float32 [768], P(('head', 'blk'))
- second_shift_grad: float32 [768], P(('head', 'blk'))
Inputs may be any that keep to these rules, and one draw needn't show every extreme that they name: `random_blocks`: each id lies within 32 blocks of its query block, counted cyclically over the 256 blocks, and for every head both ends of that reach occur. `doc_lengths`: the lengths sum to 16384.
All inputs are finite; a program needn't handle non-finite values.
Results may differ from a plain program's by a relative error of at most 0.014.
Values may be sent and summed in bfloat16 or wider, within the bound.
No kernel may reach another device: no remote copies, remote signals or barrier semaphores. Data moves between devices by JAX's collectives and lax.ppermute only.
A program may use at most 256 MiB of HBM per device.

v0:
```python
from functools import partial

import jax
import jax.numpy as jnp
from jax import lax
from jax.sharding import PartitionSpec as P

HEAD_DIM = 64
BLOCK = 64
REACH = 2


NORM_EPS = 1e-06
MASKED = -1e30
HIGH = lax.Precision.HIGHEST


def from_behind(block, axis, distance):
    devices = range(lax.axis_size(axis))
    route = [((i - distance) % len(devices), i) for i in devices]
    return lax.ppermute(block, axis, route)


def from_root(value, axis, root):
    mine = lax.axis_index(axis) == root
    return lax.psum(jnp.where(mine, value, jnp.zeros_like(value)), axis)


def slot_table(query_blocks, total, global_blocks, random_blocks):
    offsets = jnp.array([-1, 0, 1], dtype=jnp.int32)
    near = (query_blocks[:, None] + offsets[None, :]) % total
    shape = random_blocks.shape[:2]
    near = jnp.broadcast_to(near[None], shape + (3,))
    chosen = jnp.broadcast_to(global_blocks[None, None, :], shape + (global_blocks.shape[0],))
    slot_ids = jnp.concatenate([near, chosen, random_blocks], -1)
    count = slot_ids.shape[-1]
    same = slot_ids[..., :, None] == slot_ids[..., None, :]
    order = jnp.arange(count)
    earlier = order[None, :] < order[:, None]
    repeated = jnp.any(same & earlier[None, None], -1)
    return (slot_ids, jnp.logical_not(repeated))


def doc_number(positions, starts):
    return jnp.sum((positions[..., None] >= starts).astype(jnp.int32), -1)


def norm_forward(value, gain, shift):
    center = value - jnp.mean(value, -1, keepdims=True)
    spread = jnp.mean(center * center, -1, keepdims=True)
    scale_row = lax.rsqrt(spread + NORM_EPS)
    normal = center * scale_row
    return (normal * gain.astype(jnp.float32) + shift.astype(jnp.float32), normal, scale_row)


def norm_backward(grad, normal, scale_row, gain):
    gain_grad = jnp.sum(grad * normal, 0)
    shift_grad = jnp.sum(grad, 0)
    inner = grad * gain.astype(jnp.float32)
    value_grad = scale_row * (
        inner
        - jnp.mean(inner, -1, keepdims=True)
        - normal * jnp.mean(inner * normal, -1, keepdims=True)
    )
    return (value_grad, gain_grad, shift_grad)


def matmul(left, right):
    return jnp.dot(left, right, preferred_element_type=jnp.float32)


def body(
    tokens,
    cotangent,
    doc_lengths,
    global_blocks,
    random_blocks,
    query_weight,
    query_bias,
    key_weight,
    value_weight,
    value_bias,
    output_weight,
    output_bias,
    first_gain,
    first_shift,
    up_weight,
    up_bias,
    down_weight,
    down_bias,
    second_gain,
    second_shift,
):
    full = (
        lax.all_gather(query_weight, ("head", "blk"), axis=0, tiled=True),
        lax.all_gather(query_bias, ("head", "blk"), axis=0, tiled=True),
        lax.all_gather(key_weight, ("head", "blk"), axis=0, tiled=True),
        lax.all_gather(value_weight, ("head", "blk"), axis=0, tiled=True),
        lax.all_gather(value_bias, ("head", "blk"), axis=0, tiled=True),
        lax.all_gather(output_weight, ("head", "blk"), axis=0, tiled=True),
        lax.all_gather(output_bias, ("head", "blk"), axis=0, tiled=True),
        lax.all_gather(first_gain, ("head", "blk"), axis=0, tiled=True),
        lax.all_gather(first_shift, ("head", "blk"), axis=0, tiled=True),
        lax.all_gather(up_weight, ("head", "blk"), axis=0, tiled=True),
        lax.all_gather(up_bias, ("head", "blk"), axis=0, tiled=True),
        lax.all_gather(down_weight, ("head", "blk"), axis=0, tiled=True),
        lax.all_gather(down_bias, ("head", "blk"), axis=0, tiled=True),
        lax.all_gather(second_gain, ("head", "blk"), axis=0, tiled=True),
        lax.all_gather(second_shift, ("head", "blk"), axis=0, tiled=True),
    )
    (
        w_query,
        b_query,
        w_key,
        w_value,
        b_value,
        w_output,
        b_output,
        gain_one,
        shift_one,
        w_up,
        b_up,
        w_down,
        b_down,
        gain_two,
        shift_two,
    ) = full
    tok_rows, width = tokens.shape
    groups = lax.axis_size("head")
    local_width = width // groups
    local_heads = local_width // HEAD_DIM
    scale = HEAD_DIM ** (-0.5)
    query_rows = matmul(tokens, w_query) + b_query.astype(jnp.float32)
    key_rows = matmul(tokens, w_key)
    value_rows = matmul(tokens, w_value) + b_value.astype(jnp.float32)
    packed = (
        jnp.stack([query_rows, key_rows, value_rows], 1)
        .astype(jnp.bfloat16)
        .reshape(tok_rows, 3, groups, local_width)
    )
    moved = lax.all_to_all(packed, "head", split_axis=2, concat_axis=0, tiled=True)
    rows = moved.shape[0]
    per_dev = rows // BLOCK
    axis_count = lax.axis_size("blk")
    total = axis_count * per_dev
    position = lax.axis_index("blk")
    query_heads = (
        moved[:, 0, 0].reshape(per_dev, BLOCK, local_heads, HEAD_DIM).transpose(2, 0, 1, 3)
    )
    key_local = moved[:, 1, 0].reshape(rows, local_heads, HEAD_DIM)
    value_local = moved[:, 2, 0].reshape(rows, local_heads, HEAD_DIM)
    shard = jnp.concatenate([key_local, value_local], -1).reshape(
        per_dev, BLOCK, local_heads, 2 * HEAD_DIM
    )
    query_blocks = position * per_dev + jnp.arange(per_dev, dtype=jnp.int32)
    slot_ids, slot_valid = slot_table(query_blocks, total, global_blocks, random_blocks)
    slot_count = slot_ids.shape[-1]
    global_count = global_blocks.shape[0]
    slot_order = jnp.arange(slot_count)
    far_slot = (slot_order < 3) | (slot_order >= 3 + global_count)

    def pick(base):
        local = (slot_ids - base) % total
        return (local[..., None] == jnp.arange(per_dev)) & far_slot[None, None, :, None]

    def fill(piece, base):
        onehot = pick(base).astype(jnp.bfloat16)
        return jnp.einsum(
            "hqsb,bthc->hqstc", onehot, piece, preferred_element_type=jnp.float32
        ).astype(jnp.bfloat16)

    slots = fill(shard, position * per_dev)
    lower = shard
    higher = shard
    for step in range(1, REACH + 1):
        lower = from_behind(lower, "blk", 1)
        slots = slots + fill(lower, (position - step) % axis_count * per_dev)
        higher = from_behind(higher, "blk", -1)
        slots = slots + fill(higher, (position + step) % axis_count * per_dev)
    for which in range(global_count):
        block_id = global_blocks[which]
        piece = lax.dynamic_index_in_dim(shard, block_id % per_dev, 0, keepdims=False)
        arrived = from_root(piece, "blk", block_id // per_dev)
        spread_piece = jnp.broadcast_to(
            arrived.transpose(1, 0, 2)[:, None], (local_heads, per_dev, BLOCK, 2 * HEAD_DIM)
        )
        slots = slots.at[:, :, 3 + which].set(spread_piece)
    span = slot_count * BLOCK
    key_slots = slots[..., :HEAD_DIM].reshape(local_heads, per_dev, span, HEAD_DIM)
    value_slots = slots[..., HEAD_DIM:].reshape(local_heads, per_dev, span, HEAD_DIM)
    starts = jnp.cumsum(doc_lengths) - doc_lengths
    query_doc = doc_number(
        query_blocks[:, None] * BLOCK + jnp.arange(BLOCK, dtype=jnp.int32)[None, :], starts
    )
    key_doc = doc_number(
        slot_ids[..., None] * BLOCK + jnp.arange(BLOCK, dtype=jnp.int32), starts
    ).reshape(local_heads, per_dev, span)
    allowed = jnp.repeat(slot_valid, BLOCK, -1)[:, :, None, :] & (
        query_doc[None, :, :, None] == key_doc[:, :, None, :]
    )

    def scores_of():
        raw = (
            jnp.einsum(
                "hqtd,hqsd->hqts", query_heads, key_slots, preferred_element_type=jnp.float32
            )
            * scale
        )
        return jnp.where(allowed, raw, MASKED)

    scores = scores_of()
    top = jnp.max(scores, -1, keepdims=True)
    weights = jnp.exp(scores - top)
    weight_sum = jnp.sum(weights, -1, keepdims=True)
    probs = weights / weight_sum
    log_total = top + jnp.log(weight_sum)
    context = jnp.einsum(
        "hqts,hqsd->hqtd",
        probs.astype(jnp.bfloat16),
        value_slots,
        preferred_element_type=jnp.float32,
    )
    context_rows = context.astype(jnp.bfloat16).transpose(1, 2, 0, 3).reshape(rows, local_width)
    context_tok = lax.all_to_all(context_rows, "head", split_axis=0, concat_axis=1, tiled=True)
    first_sum = (
        tokens.astype(jnp.float32) + matmul(context_tok, w_output) + b_output.astype(jnp.float32)
    )
    first, first_normal, first_scale = norm_forward(first_sum, gain_one, shift_one)
    first_low = first.astype(jnp.bfloat16)
    hidden = matmul(first_low, w_up) + b_up.astype(jnp.float32)
    active, gelu_back = jax.vjp(partial(jax.nn.gelu, approximate=True), hidden)
    active_low = active.astype(jnp.bfloat16)
    second_sum = first + matmul(active_low, w_down) + b_down.astype(jnp.float32)
    result, second_normal, second_scale = norm_forward(second_sum, gain_two, shift_two)
    second_grad, gain_two_grad, shift_two_grad = norm_backward(
        cotangent.astype(jnp.float32), second_normal, second_scale, gain_two
    )
    branch_grad = second_grad.astype(jnp.bfloat16)
    down_weight_grad = matmul(active_low.T, branch_grad)
    down_bias_grad = jnp.sum(branch_grad.astype(jnp.float32), 0)
    (hidden_grad,) = gelu_back(matmul(branch_grad, w_down.T))
    hidden_low = hidden_grad.astype(jnp.bfloat16)
    up_weight_grad = matmul(first_low.T, hidden_low)
    up_bias_grad = jnp.sum(hidden_low.astype(jnp.float32), 0)
    first_grad_in = second_grad + matmul(hidden_low, w_up.T)
    first_grad, gain_one_grad, shift_one_grad = norm_backward(
        first_grad_in, first_normal, first_scale, gain_one
    )
    attended_grad = first_grad.astype(jnp.bfloat16)
    output_weight_grad = matmul(context_tok.T, attended_grad)
    output_bias_grad = jnp.sum(attended_grad.astype(jnp.float32), 0)
    context_grad = matmul(attended_grad, w_output.T).astype(jnp.bfloat16)
    context_grad_rows = lax.all_to_all(
        context_grad, "head", split_axis=1, concat_axis=0, tiled=True
    )
    context_grad_heads = context_grad_rows.reshape(per_dev, BLOCK, local_heads, HEAD_DIM).transpose(
        2, 0, 1, 3
    )
    again = jnp.exp(scores_of() - log_total)
    again_low = again.astype(jnp.bfloat16)
    prob_grad = jnp.einsum(
        "hqtd,hqsd->hqts", context_grad_heads, value_slots, preferred_element_type=jnp.float32
    )
    row_inner = jnp.sum(again * prob_grad, -1, keepdims=True)
    score_grad = (again * (prob_grad - row_inner)).astype(jnp.bfloat16)
    query_grad = (
        jnp.einsum("hqts,hqsd->hqtd", score_grad, key_slots, preferred_element_type=jnp.float32)
        * scale
    )
    key_slot_grad = (
        jnp.einsum("hqts,hqtd->hqsd", score_grad, query_heads, preferred_element_type=jnp.float32)
        * scale
    )
    value_slot_grad = jnp.einsum(
        "hqts,hqtd->hqsd", again_low, context_grad_heads, preferred_element_type=jnp.float32
    )
    slot_grad = jnp.concatenate(
        [
            key_slot_grad.reshape(local_heads, per_dev, slot_count, BLOCK, HEAD_DIM),
            value_slot_grad.reshape(local_heads, per_dev, slot_count, BLOCK, HEAD_DIM),
        ],
        -1,
    )

    def spread(base):
        onehot = pick(base).astype(jnp.float32)
        return jnp.einsum("hqsb,hqstc->bthc", onehot, slot_grad, precision=HIGH)

    upward = spread((position + REACH) % axis_count * per_dev)
    for step in range(REACH - 1, -1, -1):
        upward = from_behind(upward.astype(jnp.bfloat16), "blk", 1).astype(upward.dtype) + spread(
            (position + step) % axis_count * per_dev
        )
    downward = spread((position - REACH) % axis_count * per_dev)
    for step in range(REACH - 1, -1, -1):
        arrived_down = from_behind(downward.astype(jnp.bfloat16), "blk", -1).astype(downward.dtype)
        downward = (
            arrived_down + spread((position - step) % axis_count * per_dev)
            if step > 0
            else arrived_down
        )
    shard_grad = upward + downward
    global_terms = jnp.sum(slot_grad[:, :, 3 : 3 + global_count], 1).transpose(1, 2, 0, 3)
    global_sums = lax.psum(global_terms, "blk")
    for which in range(global_count):
        block_id = global_blocks[which]
        owned = (jnp.arange(per_dev) == block_id % per_dev) & (block_id // per_dev == position)
        shard_grad = (
            shard_grad + owned.astype(jnp.float32)[:, None, None, None] * global_sums[which][None]
        )
    key_grad_rows = shard_grad[..., :HEAD_DIM].reshape(rows, local_width)
    value_grad_rows = shard_grad[..., HEAD_DIM:].reshape(rows, local_width)
    query_grad_rows = query_grad.transpose(1, 2, 0, 3).reshape(rows, local_width)
    packed_grad = (
        jnp.stack([query_grad_rows, key_grad_rows, value_grad_rows], 1)
        .astype(jnp.bfloat16)
        .reshape(rows, 3, 1, local_width)
    )
    returned = lax.all_to_all(packed_grad, "head", split_axis=0, concat_axis=2, tiled=True).reshape(
        tok_rows, 3, width
    )
    query_low = returned[:, 0]
    key_low = returned[:, 1]
    value_low = returned[:, 2]
    query_weight_grad = matmul(tokens.T, query_low)
    query_bias_grad = jnp.sum(query_low.astype(jnp.float32), 0)
    key_weight_grad = matmul(tokens.T, key_low)
    value_weight_grad = matmul(tokens.T, value_low)
    value_bias_grad = jnp.sum(value_low.astype(jnp.float32), 0)
    tokens_grad = (
        first_grad
        + matmul(query_low, w_query.T)
        + matmul(key_low, w_key.T)
        + matmul(value_low, w_value.T)
    )
    every_grad = (
        query_weight_grad,
        query_bias_grad,
        key_weight_grad,
        value_weight_grad,
        value_bias_grad,
        output_weight_grad,
        output_bias_grad,
        gain_one_grad,
        shift_one_grad,
        up_weight_grad,
        up_bias_grad,
        down_weight_grad,
        down_bias_grad,
        gain_two_grad,
        shift_two_grad,
    )
    shares = (
        lax.psum_scatter(every_grad[0], ("head", "blk"), scatter_dimension=0, tiled=True),
        lax.psum_scatter(every_grad[1], ("head", "blk"), scatter_dimension=0, tiled=True),
        lax.psum_scatter(every_grad[2], ("head", "blk"), scatter_dimension=0, tiled=True),
        lax.psum_scatter(every_grad[3], ("head", "blk"), scatter_dimension=0, tiled=True),
        lax.psum_scatter(every_grad[4], ("head", "blk"), scatter_dimension=0, tiled=True),
        lax.psum_scatter(every_grad[5], ("head", "blk"), scatter_dimension=0, tiled=True),
        lax.psum_scatter(every_grad[6], ("head", "blk"), scatter_dimension=0, tiled=True),
        lax.psum_scatter(every_grad[7], ("head", "blk"), scatter_dimension=0, tiled=True),
        lax.psum_scatter(every_grad[8], ("head", "blk"), scatter_dimension=0, tiled=True),
        lax.psum_scatter(every_grad[9], ("head", "blk"), scatter_dimension=0, tiled=True),
        lax.psum_scatter(every_grad[10], ("head", "blk"), scatter_dimension=0, tiled=True),
        lax.psum_scatter(every_grad[11], ("head", "blk"), scatter_dimension=0, tiled=True),
        lax.psum_scatter(every_grad[12], ("head", "blk"), scatter_dimension=0, tiled=True),
        lax.psum_scatter(every_grad[13], ("head", "blk"), scatter_dimension=0, tiled=True),
        lax.psum_scatter(every_grad[14], ("head", "blk"), scatter_dimension=0, tiled=True),
    )
    return (
        result.astype(jnp.bfloat16),
        tokens_grad,
        shares[0],
        shares[1],
        shares[2],
        shares[3],
        shares[4],
        shares[5],
        shares[6],
        shares[7],
        shares[8],
        shares[9],
        shares[10],
        shares[11],
        shares[12],
        shares[13],
        shares[14],
    )


def solution(mesh):
    return jax.shard_map(
        body,
        mesh=mesh,
        in_specs=(
            P(("blk", "head"), None),
            P(("blk", "head"), None),
            P(),
            P(),
            P("head", "blk", None),
            P(("head", "blk"), None),
            P(("head", "blk")),
            P(("head", "blk"), None),
            P(("head", "blk"), None),
            P(("head", "blk")),
            P(("head", "blk"), None),
            P(("head", "blk")),
            P(("head", "blk")),
            P(("head", "blk")),
            P(("head", "blk"), None),
            P(("head", "blk")),
            P(("head", "blk"), None),
            P(("head", "blk")),
            P(("head", "blk")),
            P(("head", "blk")),
        ),
        out_specs=(
            P(("blk", "head"), None),
            P(("blk", "head"), None),
            P(("head", "blk"), None),
            P(("head", "blk")),
            P(("head", "blk"), None),
            P(("head", "blk"), None),
            P(("head", "blk")),
            P(("head", "blk"), None),
            P(("head", "blk")),
            P(("head", "blk")),
            P(("head", "blk")),
            P(("head", "blk"), None),
            P(("head", "blk")),
            P(("head", "blk"), None),
            P(("head", "blk")),
            P(("head", "blk")),
            P(("head", "blk")),
        ),
        check_vma=False,
    )
```

profile of v0, /device:TPU:0, one launch (start us, length us, event | category | flops | bytes accessed | tf_op | source)
XLA Modules:
  0.0 1662.4 jit_solution(1349499109532081287)
XLA Ops:
  17.0 42.7 %all-reduce.19 = (bf16[768]{0:T(1024)(128)(2,1)S(1)}, bf16[768]{0:T(1024)(128)(2,1)S(1)}, bf16[768]{0:T(1024)(128)(2,1)}, bf16[768]{0:T(1024)(128)(2,1)}, bf16[7...) all-reduce(bf16[768]{0:T(1024)(128)(2,1)S(1)} %dynamic-update-slice, ...), channel_id=1, replica_groups=mesh['head'=2,'blk'=16] {'head','blk'}, use_global_device_ids=true, to_apply=%add.1 | all-reduce | flops 9216 | bytes 36864
  70.6 53.1 %all-gather.11.cloned.1.call-done = bf16[768,768]{1,0:T(8,128)(2,1)} async-done(((bf16[24,768]{1,0:T(8,128)(2,1)}), bf16[768,768]{1,0:T(8,128)(2,1)}) %all-gather.11.cloned.1.call-update) | async-done | bytes 1179664 | tf_op jit(solution)/shard_map/all_gather | solution.py:98
  126.0 53.5 %all-gather.9.cloned.1.call-done = bf16[768,768]{1,0:T(8,128)(2,1)} async-done(((bf16[24,768]{1,0:T(8,128)(2,1)}), bf16[768,768]{1,0:T(8,128)(2,1)}) %all-gather.9.cloned.1.call-update) | async-done | bytes 1179664 | tf_op jit(solution)/shard_map/all_gather | solution.py:97
  193.4 22.5 %all-to-all-done = bf16[512,3,2,384]{3,0,1,2:T(8,128)(2,1)S(1)} async-done(((bf16[512,3,2,384]{3,0,1,2:T(8,128)(2,1)}), bf16[512,3,2,384]{3,0,1,2:T(8,128)(2,1)S(1)}, u32[]{:S(2)}, u32[]{:S(2)}) %all-to-all-start) | async-done | bytes 2359328 | tf_op jit(solution)/shard_map/all_to_all | solution.py:141
  297.5 22.4 %convert_add_fusion = bf16[6,16,8,64,128]{4,2,3,1,0:T(8,128)(2,1)} fusion(bf16[6,16,8,64,128]{4,2,3,1,0:T(8,128)(2,1)} %fusion.28, bf16[6,16,8,64,128]{4,2,3,1,0:T(8,128)(2,1)} %fusion.30, bf16[6,16,8,64,128]{4,2,3,1,0:T(8,128)(2,1)} %fusion.32, bf16[6,16,8,64,128]{4,2,3,1,0:T(8,128)(2,1)} %fusion.34, pred[6,16,8,16,1]{3,2,4,1,0:T(8,128)(4,1)S(1)} %copy-done.17, ...), kind=kOutput, calls=%fused_computation.7 | convolution fusion | flops 232783872 | bytes 64499712 | tf_op jit(solution)/shard_map/hqsb,bthc->hqstc/dot_general | solution.py:168
  332.3 75.9 %scatter.6 = bf16[6,16,8,64,128]{4,2,3,1,0:T(8,128)(2,1)} dynamic-update-slice(bf16[6,16,8,64,128]{4,2,3,1,0:T(8,128)(2,1)} %convert_add_fusion, bf16[6,16,1,64,128]{4,2,3,1,0:T(2,128)(2,1)S(1)} %broadcast.504, s32[]{:T(128)} %constant.227.clone.1, s32[]{:T(128)} %constant.227.clone.1, s32[]{:T(128)} %constant.232.clone.1, s32[]{:T(128)} %constant.227.clone.1, s32[]{:T(128)} %constant.227.clone.1) | dynamic-update-slice | bytes 3145732 | tf_op jit(solution)/shard_map/scatter | solution.py:187
  411.1 75.8 %scatter.9 = bf16[6,16,8,64,128]{4,2,3,1,0:T(8,128)(2,1)} dynamic-update-slice(bf16[6,16,8,64,128]{4,2,3,1,0:T(8,128)(2,1)} %scatter.6, bf16[6,16,1,64,128]{4,2,3,1,0:T(2,128)(2,1)S(1)} %broadcast.505, s32[]{:T(128)} %constant.227.clone.1, s32[]{:T(128)} %constant.227.clone.1, s32[]{:T(128)} %constant.239.clone.1, s32[]{:T(128)} %constant.227.clone.1, s32[]{:T(128)} %constant.227.clone.1) | dynamic-update-slice | bytes 3145732 | tf_op jit(solution)/shard_map/scatter | solution.py:187
  487.0 19.5 %fusion.112 = (bf16[6,16,8,64,64]{4,2,3,1,0:T(8,128)(2,1)}, bf16[6,16,8,64,64]{4,2,3,1,0:T(8,128)(2,1)}) fusion(bf16[6,16,8,64,128]{4,2,3,1,0:T(8,128)(2,1)} %scatter.9), kind=kLoop, calls=%fused_computation.213 | loop fusion | bytes 25165824 | tf_op jit(solution)/shard_map/slice | solution.py:189
  506.5 18.2 %copy.190 = bf16[6,16,8,64,64]{3,2,4,1,0:T(8,128)(2,1)} copy(bf16[6,16,8,64,64]{4,2,3,1,0:T(8,128)(2,1)} %get-tuple-element.158) | data formatting | bytes 12582912 | tf_op jit(solution)/shard_map/slice | solution.py:189
  524.7 17.3 %reshape.581 = bf16[6,16,512,64]{2,3,1,0:T(8,128)(2,1)} reshape(bf16[6,16,8,64,64]{3,2,4,1,0:T(8,128)(2,1)} %copy.190) | data formatting | bytes 12582912 | tf_op jit(solution)/shard_map/reshape | solution.py:189
  541.9 18.0 %copy.191 = bf16[6,16,8,64,64]{3,2,4,1,0:T(8,128)(2,1)} copy(bf16[6,16,8,64,64]{4,2,3,1,0:T(8,128)(2,1)} %get-tuple-element.159) | data formatting | bytes 12582912 | tf_op jit(solution)/shard_map/slice | solution.py:190
  708.6 18.9 %reshape.584 = f32[6,16,8,64,64]{3,2,4,1,0:T(8,128)} reshape(f32[6,16,512,64]{2,3,1,0:T(8,128)} %broadcast_multiply_fusion) | data formatting | bytes 25165824 | tf_op jit(solution)/shard_map/reshape | solution.py:279
  727.4 27.1 %copy.200 = f32[6,16,8,64,64]{4,1,2,3,0:T(8,128)} copy(f32[6,16,8,64,64]{3,2,4,1,0:T(8,128)} %reshape.584) | data formatting | bytes 25165824 | tf_op jit(solution)/shard_map/reshape | solution.py:279
  754.5 18.9 %reshape.585 = f32[6,16,8,64,64]{3,2,4,1,0:T(8,128)} reshape(f32[6,16,512,64]{2,3,1,0:T(8,128)} %fusion.9) | data formatting | bytes 25165824 | tf_op jit(solution)/shard_map/reshape | solution.py:280
  773.4 27.0 %copy.201 = f32[6,16,8,64,64]{4,1,2,3,0:T(8,128)} copy(f32[6,16,8,64,64]{3,2,4,1,0:T(8,128)} %reshape.585) | data formatting | bytes 25165824 | tf_op jit(solution)/shard_map/reshape | solution.py:280
  868.7 19.7 %collective-permute-start.5 = (bf16[16,64,6,128]{3,0,1,2:T(8,128)(2,1)}, bf16[16,64,6,128]{3,0,1,2:T(8,128)(2,1)}, u32[]{:S(2)}, u32[]{:S(2)}) collective-permute-start(bf16[16,64,6,128]{3,0,1,2:T(8,128)(2,1)} %fusion.18), channel_id=1, source_target_pairs={{15,0},{0,1},{1,2},{2,3},{3,4},{4,5},{5,6},{6,7},{7,8},{8,9},{9,10... | collective-permute-start | bytes 4718600 | tf_op jit(solution)/shard_map/ppermute | solution.py:21
  922.5 30.0 %all-reduce.24.cloned.1.call-done = f32[2,64,6,128]{3,0,1,2:T(2,128)} async-done(((f32[2,64,6,128]{3,0,1,2:T(2,128)}), f32[2,64,6,128]{3,0,1,2:T(2,128)}) %all-reduce.24.cloned.1.call-update) | async-done | bytes 393232 | tf_op jit(solution)/shard_map/psum | solution.py:304
  975.9 42.5 %all_to_all.68 = bf16[1024,3,1,384]{3,1,2,0:T(4,128)(2,1)S(1)} all-to-all(bf16[1024,3,1,384]{3,1,2,0:T(4,128)(2,1)S(1)} %copy.204), channel_id=1, replica_groups=mesh['head'=2,'blk'=16] {'head'}, dimensions={0} | all-to-all | bytes 4718592 | tf_op jit(solution)/shard_map/all_to_all | solution.py:319
  1066.6 39.1 %all-reduce.18 = (f32[768]{0:T(1024)S(1)}, f32[768]{0:T(1024)S(1)}, f32[768]{0:T(1024)S(1)}, f32[768]{0:T(1024)S(1)}, f32[768]{0:T(1024)S(1)}, /*index=5*/f32[30...) all-reduce(f32[768]{0:T(1024)S(1)} %convert_reduce_fusion.6, ...), channel_id=3, replica_groups=mesh['head'=2,'blk'=16] {'head','blk'}, use_global_device_ids=true, to_apply=%region_21.22.clone | all-reduce | flops 9216 | bytes 73728
  1116.9 47.2 %reduce-scatter.19.cloned.1.call-done = f32[24,768]{1,0:T(8,128)} async-done(((f32[768,768]{1,0:T(8,128)}), f32[24,768]{1,0:T(8,128)}) %reduce-scatter.19.cloned.1.call-update) | async-done | bytes 73744
  1164.1 104.8 %reduce-scatter.23.cloned.1.call-done = f32[24,768]{1,0:T(8,128)} async-done(((f32[768,768]{1,0:T(8,128)}), f32[24,768]{1,0:T(8,128)}) %reduce-scatter.23.cloned.1.call-update) | async-done | bytes 73744
  1268.9 103.8 %reduce-scatter.21.cloned.1.call-done = f32[24,768]{1,0:T(8,128)} async-done(((f32[768,768]{1,0:T(8,128)}), f32[24,768]{1,0:T(8,128)}) %reduce-scatter.21.cloned.1.call-update) | async-done | bytes 73744
  1372.7 142.1 %reduce-scatter.17.cloned.1.call-done = f32[96,768]{1,0:T(8,128)} async-done(((f32[3072,768]{1,0:T(8,128)}), f32[96,768]{1,0:T(8,128)}) %reduce-scatter.17.cloned.1.call-update) | async-done | bytes 294928 | tf_op jit(solution)/shard_map/reduce_scatter | solution.py:365
  1514.8 140.8 %reduce-scatter.15.cloned.1.call-done = f32[24,3072]{1,0:T(8,128)} async-done(((f32[768,3072]{1,0:T(8,128)}), f32[24,3072]{1,0:T(8,128)}) %reduce-scatter.15.cloned.1.call-update) | async-done | bytes 294928 | tf_op jit(solution)/shard_map/reduce_scatter | solution.py:363
  (352 shorter events, 461.2 us)
Async XLA Ops:
  7.2 60.8 %all-gather.7.cloned.1.call-start = ((), (), s32[]{:S(2)}) async-start(), calls=%async_computation.10 | async-start | bytes 1216512 | tf_op jit(solution)/shard_map/all_gather | solution.py:95
  7.9 115.7 %all-gather.11.cloned.1.call-start = ((), (), s32[]{:S(2)}) async-start(), calls=%async_computation.12 | async-start | bytes 1216512 | tf_op jit(solution)/shard_map/all_gather | solution.py:98
  8.7 170.8 %all-gather.9.cloned.1.call-start = ((), (), s32[]{:S(2)}) async-start(), calls=%async_computation.11 | async-start | bytes 1216512 | tf_op jit(solution)/shard_map/all_gather | solution.py:97
  183.6 32.3 %all-to-all-start = ((bf16[512,3,2,384]{3,0,1,2:T(8,128)(2,1)}), bf16[512,3,2,384]{3,0,1,2:T(8,128)(2,1)S(1)}, u32[]{:S(2)}, u32[]{:S(2)}) async-start(bf16[512,3,2,384]{3,0,1,2:T(8,128)(2,1)} %pad_maximum_fusion.1), calls=%async_computation | async-start | bytes 4718592 | tf_op jit(solution)/shard_map/all_to_all | solution.py:141
  187.5 140.9 %all-reduce.26.cloned.1.call-start = ((), (), s32[]{:S(2)}) async-start(), calls=%async_computation.23 | async-start | bytes 393216 | tf_op jit(solution)/shard_map/psum | solution.py:26
  228.9 373.0 %all-gather.13.cloned.1.call-start = ((), (), s32[]{:S(2)}) async-start(), calls=%async_computation.13 | async-start | bytes 1216512 | tf_op jit(solution)/shard_map/all_gather | solution.py:100
  229.5 383.0 %all-gather.15.cloned.1.call-start = ((), (), s32[]{:S(2)}) async-start(), calls=%async_computation.14 | async-start | bytes 4866048 | tf_op jit(solution)/shard_map/all_gather | solution.py:104
  230.1 389.8 %all-gather.17.cloned.1.call-start = ((), (), s32[]{:S(2)}) async-start(), calls=%async_computation.15 | async-start | bytes 4866048 | tf_op jit(solution)/shard_map/all_gather | solution.py:106
  233.7 23.9 %collective-permute-start = (bf16[16,64,6,128]{3,0,1,2:T(8,128)(2,1)}, bf16[16,64,6,128]{3,0,1,2:T(8,128)(2,1)S(1)}, u32[]{:S(2)}, u32[]{:S(2)}) collective-permute-start(bf16[16,64,6,128]{3,0,1,2:T(8,128)(2,1)} %pad_maximum_fusion.3), channel_id=1, source_target_pairs={{15,0},{0,1},{1,2},{2,3},{3,4},{4,5},{5,6},{6,7},{7,8},{8,9},{9,10... | collective-permute-start | bytes 4718600 | tf_op jit(solution)/shard_map/ppermute | solution.py:21
  236.2 41.9 %collective-permute-start.1 = (bf16[16,64,6,128]{3,0,1,2:T(8,128)(2,1)}, bf16[16,64,6,128]{3,0,1,2:T(8,128)(2,1)S(1)}, u32[]{:S(2)}, u32[]{:S(2)}) collective-permute-start(bf16[16,64,6,128]{3,0,1,2:T(8,128)(2,1)} %pad_maximum_fusion.3), channel_id=1, source_target_pairs={{1,0},{2,1},{3,2},{4,3},{5,4},{6,5},{7,6},{8,7},{9,8},{10,9},{11,1... | collective-permute-start | bytes 4718600 | tf_op jit(solution)/shard_map/ppermute | solution.py:21
  257.6 33.5 %collective-permute-start.2 = (bf16[16,64,6,128]{3,0,1,2:T(8,128)(2,1)S(1)}, bf16[16,64,6,128]{3,0,1,2:T(8,128)(2,1)S(1)}, u32[]{:S(2)}, u32[]{:S(2)}) collective-permute-start(bf16[16,64,6,128]{3,0,1,2:T(8,128)(2,1)S(1)} %collective-permute-done), channel_id=1, source_target_pairs={{15,0},{0,1},{1,2},{2,3},{3,4},{4,5},{5,6},{6,7},{7,8},{8,9},{9,10... | collective-permute-start | bytes 4718600 | tf_op jit(solution)/shard_map/ppermute | solution.py:21
  278.1 19.4 %collective-permute-start.3 = (bf16[16,64,6,128]{3,0,1,2:T(8,128)(2,1)S(1)}, bf16[16,64,6,128]{3,0,1,2:T(8,128)(2,1)}, u32[]{:S(2)}, u32[]{:S(2)}) collective-permute-start(bf16[16,64,6,128]{3,0,1,2:T(8,128)(2,1)S(1)} %collective-permute-done.1), channel_id=1, source_target_pairs={{1,0},{2,1},{3,2},{4,3},{5,4},{6,5},{7,6},{8,7},{9,8},{10,9},{11,1... | collective-permute-start | bytes 4718600 | tf_op jit(solution)/shard_map/ppermute | solution.py:21
  598.1 11.5 all-to-all-start.1
  650.5 302.0 %all-reduce.24.cloned.1.call-start = ((), (), s32[]{:S(2)}) async-start(), calls=%async_computation.16 | async-start | bytes 786432 | tf_op jit(solution)/shard_map/psum | solution.py:304
  826.8 25.1 %collective-permute-start.4 = (bf16[16,64,6,128]{3,0,1,2:T(8,128)(2,1)}, bf16[16,64,6,128]{3,0,1,2:T(8,128)(2,1)}, u32[]{:S(2)}, u32[]{:S(2)}) collective-permute-start(bf16[16,64,6,128]{3,0,1,2:T(8,128)(2,1)} %fusion.44), channel_id=1, source_target_pairs={{15,0},{0,1},{1,2},{2,3},{3,4},{4,5},{5,6},{6,7},{7,8},{8,9},{9,10... | collective-permute-start | bytes 4718600 | tf_op jit(solution)/shard_map/ppermute | solution.py:21
  841.4 47.0 %collective-permute-start.6 = (bf16[16,64,6,128]{3,0,1,2:T(8,128)(2,1)}, bf16[16,64,6,128]{3,0,1,2:T(8,128)(2,1)}, u32[]{:S(2)}, u32[]{:S(2)}) collective-permute-start(bf16[16,64,6,128]{3,0,1,2:T(8,128)(2,1)} %fusion.45), channel_id=1, source_target_pairs={{1,0},{2,1},{3,2},{4,3},{5,4},{6,5},{7,6},{8,7},{9,8},{10,9},{11,1... | collective-permute-start | bytes 4718600 | tf_op jit(solution)/shard_map/ppermute | solution.py:21
  849.5 267.3 %reduce-scatter.13.cloned.1.call-start = ((), (), s32[]{:S(2)}) async-start(), calls=%async_computation.17 | async-start | bytes 2433024 | tf_op jit(solution)/shard_map/reduce_scatter | solution.py:359
  851.9 312.2 %reduce-scatter.19.cloned.1.call-start = ((), (), s32[]{:S(2)}) async-start(), calls=%async_computation.20 | async-start | bytes 2433024
  868.7 85.3 %collective-permute-start.5 = (bf16[16,64,6,128]{3,0,1,2:T(8,128)(2,1)}, bf16[16,64,6,128]{3,0,1,2:T(8,128)(2,1)}, u32[]{:S(2)}, u32[]{:S(2)}) collective-permute-start(bf16[16,64,6,128]{3,0,1,2:T(8,128)(2,1)} %fusion.18), channel_id=1, source_target_pairs={{15,0},{0,1},{1,2},{2,3},{3,4},{4,5},{5,6},{6,7},{7,8},{8,9},{9,10... | collective-permute-start | bytes 4718600 | tf_op jit(solution)/shard_map/ppermute | solution.py:21
  899.1 54.9 %collective-permute-start.7 = (bf16[16,64,6,128]{3,0,1,2:T(8,128)(2,1)}, bf16[16,64,6,128]{3,0,1,2:T(8,128)(2,1)}, u32[]{:S(2)}, u32[]{:S(2)}) collective-permute-start(bf16[16,64,6,128]{3,0,1,2:T(8,128)(2,1)} %fusion.13), channel_id=1, source_target_pairs={{1,0},{2,1},{3,2},{4,3},{5,4},{6,5},{7,6},{8,7},{9,8},{10,9},{11,1... | collective-permute-start | bytes 4718600 | tf_op jit(solution)/shard_map/ppermute | solution.py:21
  1028.5 240.4 %reduce-scatter.23.cloned.1.call-start = ((), (), s32[]{:S(2)}) async-start(), calls=%async_computation.22 | async-start | bytes 2433024
  1033.8 338.9 %reduce-scatter.21.cloned.1.call-start = ((), (), s32[]{:S(2)}) async-start(), calls=%async_computation.21 | async-start | bytes 2433024
  1039.2 475.7 %reduce-scatter.17.cloned.1.call-start = ((), (), s32[]{:S(2)}) async-start(), calls=%async_computation.19 | async-start | bytes 9732096 | tf_op jit(solution)/shard_map/reduce_scatter | solution.py:365
  1050.5 605.1 %reduce-scatter.15.cloned.1.call-start = ((), (), s32[]{:S(2)}) async-start(), calls=%async_computation.18 | async-start | bytes 9732096 | tf_op jit(solution)/shard_map/reduce_scatter | solution.py:363
  (67 other events, 966.0 us)
Sparse Core Ops, SparseCore 0:
  10.9 57.0 all-gather.6
  70.9 52.7 all-gather.10
  126.5 52.9 all-gather.8
  229.0 99.2 all-reduce.25
  331.1 53.0 all-gather.12
  386.9 62.4 all-gather.14
  452.4 62.4 all-gather.16
  849.7 102.7 all-reduce.23
  959.2 101.0 reduce-scatter.12
  1066.0 98.0 reduce-scatter.18
  1170.8 98.0 reduce-scatter.22
  1274.6 98.0 reduce-scatter.20
  1380.2 134.6 reduce-scatter.16
  1521.1 134.4 reduce-scatter.14
where the time goes:
time: 1680 us; the launch traced here: 1660 us
  waiting for transfers between devices  740 us (44%)
  local copies, waits for them, and re-layouts  437 us (26%)
  matrix products  225 us (13%)
  blocking collectives  124 us (7%)
  other arithmetic  61.7 us (4%)
  starting transfers between devices  54.7 us (3%)
  between operations  20.6 us (1%)
    unnamed x17, waiting for transfers between devices  260 us
    scatter x2, local copies, waits for them, and re-layouts, body(): slots = slots.at[:, :, 3 + which].set(spread_piece)  152 us
    reduce_scatter x1, waiting for transfers between devices, body(): lax.psum_scatter(every_grad[11], ('head', 'blk'), scatter_dimension=0, ti...  142 us
    reduce_scatter x1, waiting for transfers between devices, body(): lax.psum_scatter(every_grad[9], ('head', 'blk'), scatter_dimension=0, til...  141 us
    unnamed x2, blocking collectives  81.8 us
    dot_general x18, matrix products, matmul(): return jnp.dot(left, right, preferred_element_type=jnp.float32)  68.9 us
    dot_general x5, matrix products, spread(): return jnp.einsum('hqsb,hqstc->bthc', onehot, slot_grad, precision=HIGH)  54.5 us
    all_gather x1, waiting for transfers between devices, body(): lax.all_gather(key_weight, ('head', 'blk'), axis=0, tiled=True)  53.5 us
  transfers between devices with their start and end apart: 25, of which 14 were waited for; matrix products, arithmetic and copies ran while one was open for 30% of the time, Pallas kernels for 0%

commit v1 on v0

v1 whole, which is shorter than its diff:
```python
from functools import partial

import jax
import jax.numpy as jnp
from jax import lax
from jax.experimental import pallas as pl
from jax.experimental.pallas import tpu as pltpu
from jax.sharding import PartitionSpec as P

HEAD_DIM = 64
BLOCK = 64
LANES = 128
NORM_EPS = 1e-06
MASKED = -1e30
AXES = ("head", "blk")
BF16 = jnp.bfloat16
F32 = jnp.float32
PAIRS = ((0, 0), (1, 0), (0, 1), (1, 1))
VMEM_LIMIT = 60 * 1024 * 1024


def matmul(left, right):
    return jnp.dot(left, right, preferred_element_type=F32)


def dot_rows(left, right):
    return lax.dot_general(left, right, (((0,), (0,)), ((), ())), preferred_element_type=F32)


def dot_lanes(left, right):
    return lax.dot_general(left, right, (((1,), (1,)), ((), ())), preferred_element_type=F32)


class Place:
    def __init__(self):
        self.size = lax.axis_size("blk")
        self.slabs = self.size // 4
        blk = lax.axis_index("blk")
        self.h = lax.axis_index("head")
        self.n = blk // 4
        self.x = (blk // 2) % 2
        self.c = blk % 2

    def send(self, value, target):
        def index(h, n, x, c):
            return h * self.size + 4 * n + 2 * x + c

        route = [
            (index(h, n, x, c), index(*target(h, n, x, c)))
            for h in range(2)
            for n in range(self.slabs)
            for x in range(2)
            for c in range(2)
        ]
        return lax.ppermute(value, AXES, route)

    def along_slabs(self, value, k):
        return self.send(value, lambda h, n, x, c: (h, n ^ k, x, c))

    def across(self, value, i, j):
        return self.send(value, lambda h, n, x, c: (h ^ i, n, x ^ j, c))

    def sibling(self, value):
        return self.send(value, lambda h, n, x, c: (h, n, x, 1 - c))

    def to_heads(self, value, i, j):
        return self.send(value, lambda h, n, x, c: (h ^ i, n, c ^ j, x))

    def to_tokens(self, value, i, j):
        return self.send(value, lambda h, n, x, c: (h ^ i, n, c, x ^ j))

    def to_next(self, value):
        def target(h, n, x, c):
            return (h, n, x, 1) if c == 0 else (h, (n + 1) % self.slabs, x, 0)

        return self.send(value, target)

    def to_previous(self, value):
        def target(h, n, x, c):
            return (h, n, x, 0) if c == 1 else (h, (n - 1) % self.slabs, x, 1)

        return self.send(value, target)


def pick(value, index, axis=0):
    return lax.dynamic_index_in_dim(value, index, axis, keepdims=False)


def assemble(place, mine, other):
    slabs, rows, columns = mine[0].shape
    pieces = list(mine) + list(other)
    where = jnp.stack([place.h, place.n, place.x, place.c]).astype(jnp.int32)

    def kernel(where_ref, *refs):
        sources, out = refs[:8], refs[8]
        h, x, c = where_ref[0], where_ref[2], where_ref[3]
        for which in range(8):
            i, j = PAIRS[which % 4]
            out[h ^ i, 0, x ^ j, c ^ (which // 4)] = sources[which][0]

    found = pl.pallas_call(
        kernel,
        out_shape=jax.ShapeDtypeStruct((2, slabs, 2, 2, rows, columns), pieces[0].dtype),
        grid_spec=pltpu.PrefetchScalarGridSpec(
            num_scalar_prefetch=1,
            grid=(slabs,),
            in_specs=[pl.BlockSpec((1, rows, columns), lambda k, w: (k, 0, 0))] * 8,
            out_specs=pl.BlockSpec(
                (2, 1, 2, 2, rows, columns), lambda k, w: (0, k ^ w[1], 0, 0, 0, 0)
            ),
        ),
        compiler_params=pltpu.CompilerParams(vmem_limit_bytes=VMEM_LIMIT),
        name="assemble",
    )(where, *pieces)
    return found.reshape(8 * slabs, rows, columns)


def gather_shards(place, value):
    column = jnp.stack([value] + [place.along_slabs(value, k) for k in range(1, place.slabs)])
    mine = [column] + [place.across(column, i, j) for i, j in PAIRS[1:]]
    other = [place.sibling(piece) for piece in mine]
    return assemble(place, mine, other)


def gather_group(place, value):
    column = jnp.stack([value] + [place.along_slabs(value, k) for k in range(1, place.slabs)])

    def part(i, j):
        return pick(column, (place.h ^ i) * 2 + (place.x ^ j), 1)

    mine = [part(0, 0)] + [place.across(part(i, j), i, j) for i, j in PAIRS[1:]]
    other = [place.sibling(piece) for piece in mine]
    return assemble(place, mine, other)


def halve(place, value):
    kept = pick(value, place.c, 3)
    sent = pick(value, 1 - place.c, 3).astype(BF16)
    return kept.astype(F32) + place.sibling(sent).astype(F32)


def scatter_sum(place, value):
    half = halve(place, value).astype(BF16)

    def part(i, j):
        return pick(pick(half, place.h ^ i), place.x ^ j, 1)

    quarter = part(0, 0).astype(F32)
    for i, j in PAIRS[1:]:
        quarter = quarter + place.across(part(i, j), i, j).astype(F32)
    low = quarter.astype(BF16)
    total = pick(quarter, place.n)
    for k in range(1, place.slabs):
        total = total + place.along_slabs(pick(low, place.n ^ k), k).astype(F32)
    return total


def scatter_group(place, value):
    half = halve(place, value).astype(BF16)
    total = pick(half, place.n, 1).astype(F32)
    for k in range(1, place.slabs):
        total = total + place.along_slabs(pick(half, place.n ^ k, 1), k).astype(F32)

    def part(i, j):
        return pick(pick(total, place.h ^ i), place.x ^ j)

    found = [part(0, 0)] + [place.across(part(i, j), i, j) for i, j in PAIRS[1:]]
    found = jnp.stack([found[0], found[2], found[1], found[3]])
    own = place.h * 2 + place.x
    return [pick(found, own ^ group) for group in range(4)]


def doc_count(position, starts_ref, count):
    total = jnp.zeros(position.shape, jnp.int32)
    for which in range(count):
        total = total + (position >= starts_ref[which]).astype(jnp.int32)
    return total


def load_slots(kv, slots_ref, base, head):
    lanes = slice(head * LANES, (head + 1) * LANES)
    return jnp.concatenate([kv[slots_ref[base + s], :, lanes] for s in range(8)], 0)


def copy_in(sources, kv, sems):
    copies = []
    for which, source in enumerate(sources):
        start = 8 * which
        copies.append(
            pltpu.make_async_copy(source, kv.at[pl.ds(start, source.shape[0])], sems.at[which])
        )
    for copy in copies:
        copy.start()
    for copy in copies:
        copy.wait()


STEP = 2


def attend_forward(slots, ids, query_ids, starts, queries, pieces):
    heads = 3
    blocks = queries.shape[0] // BLOCK
    docs = starts.shape[0]
    many = len(pieces)

    def kernel(slots_ref, ids_ref, query_ids_ref, starts_ref, q_ref, *refs):
        sources = refs[:many]
        ctx_ref, p_ref, kv, sems = refs[many:]
        step = pl.program_id(0)

        @pl.when(step == 0)
        def _():
            copy_in(sources, kv, sems)

        lane = lax.broadcasted_iota(jnp.int32, (1, LANES), 1)
        row = lax.broadcasted_iota(jnp.int32, (BLOCK, LANES), 0)
        for u in range(STEP):
            block = step * STEP + u
            query_doc = doc_count(query_ids_ref[block] * BLOCK + row, starts_ref, docs)
            contexts = []
            for head in range(heads):
                base = (head * blocks + block) * 8
                slot = load_slots(kv, slots_ref, base, head)
                q = q_ref[u * BLOCK : (u + 1) * BLOCK, head * LANES : (head + 1) * LANES]
                scores = dot_lanes(q, slot)
                tiles = []
                for tile in range(4):
                    first = ids_ref[base + 2 * tile] * BLOCK
                    second = ids_ref[base + 2 * tile + 1] * BLOCK - BLOCK
                    key_doc = doc_count(
                        jnp.where(lane < BLOCK, first + lane, second + lane), starts_ref, docs
                    )
                    tiles.append(
                        jnp.where(
                            query_doc == key_doc,
                            scores[:, tile * LANES : (tile + 1) * LANES],
                            MASKED,
                        )
                    )
                top = jnp.maximum(
                    jnp.maximum(tiles[0], tiles[1]), jnp.maximum(tiles[2], tiles[3])
                )
                top = jnp.max(top, -1, keepdims=True)
                tiles = [jnp.exp(tile - top) for tile in tiles]
                total = (tiles[0] + tiles[1]) + (tiles[2] + tiles[3])
                inverse = 1.0 / jnp.sum(total, -1, keepdims=True)
                low = jnp.concatenate([(tile * inverse).astype(BF16) for tile in tiles], 1)
                p_ref[u, head] = low
                contexts.append(matmul(low, slot))
            rows = slice(u * BLOCK, (u + 1) * BLOCK)
            ctx_ref[rows, :LANES] = jnp.where(lane < BLOCK, contexts[0], contexts[1]).astype(BF16)
            ctx_ref[rows, LANES:] = jnp.where(lane < BLOCK, contexts[2], 0.0).astype(BF16)

    return pl.pallas_call(
        kernel,
        out_shape=(
            jax.ShapeDtypeStruct((blocks * BLOCK, 2 * LANES), BF16),
            jax.ShapeDtypeStruct((blocks, heads, BLOCK, 8 * BLOCK), BF16),
        ),
        grid_spec=pltpu.PrefetchScalarGridSpec(
            num_scalar_prefetch=4,
            grid=(blocks // STEP,),
            in_specs=[pl.BlockSpec((STEP * BLOCK, heads * LANES), lambda i, *_: (i, 0))]
            + [pl.BlockSpec(memory_space=pl.ANY)] * many,
            out_specs=[
                pl.BlockSpec((STEP * BLOCK, 2 * LANES), lambda i, *_: (i, 0)),
                pl.BlockSpec((STEP, heads, BLOCK, 8 * BLOCK), lambda i, *_: (i, 0, 0, 0)),
            ],
            scratch_shapes=[
                pltpu.VMEM((3 * blocks + 2, BLOCK, heads * LANES), BF16),
                pltpu.SemaphoreType.DMA((many,)),
            ],
        ),
        compiler_params=pltpu.CompilerParams(vmem_limit_bytes=VMEM_LIMIT),
        cost_estimate=pl.CostEstimate(
            flops=20_000_000_000, bytes_accessed=20_000_000, transcendentals=3_000_000
        ),
        name="attend_forward",
    )(slots, ids, query_ids, starts, queries, *pieces)


def attend_backward(slots, queries, probs, context_grad, pieces):
    heads = 3
    blocks = queries.shape[0] // BLOCK
    many = len(pieces)

    def kernel(slots_ref, q_ref, p_ref, grad_ref, *refs):
        sources = refs[:many]
        dq_ref, own_ref, next_ref, prev_ref, glob_ref, kv, acc, sems = refs[many:]
        step = pl.program_id(0)

        @pl.when(step == 0)
        def _():
            def clear(i, _):
                acc[i] = jnp.zeros(acc.shape[1:], F32)
                return _

            lax.fori_loop(0, acc.shape[0], clear, 0)
            copy_in(sources, kv, sems)

        lane = lax.broadcasted_iota(jnp.int32, (1, LANES), 1)
        left = lane < BLOCK
        for u in range(STEP):
            block = step * STEP + u
            rows = slice(u * BLOCK, (u + 1) * BLOCK)
            for head in range(heads):
                base = (head * blocks + block) * 8
                lanes = slice(head * LANES, (head + 1) * LANES)
                slot = load_slots(kv, slots_ref, base, head)
                q = q_ref[rows, lanes]
                value_side = left if head % 2 == 0 else jnp.logical_not(left)
                tile = head // 2
                grad = grad_ref[rows, tile * LANES : (tile + 1) * LANES].astype(F32)
                grad = jnp.where(value_side, grad, 0.0).astype(BF16)
                low = p_ref[u, head]
                probs_f = low.astype(F32)
                prob_grad = dot_lanes(grad, slot)
                both = probs_f * prob_grad
                inner = jnp.sum(both, -1, keepdims=True)
                score_grad = (both - probs_f * inner).astype(BF16)
                dq = matmul(score_grad, slot)
                dq_ref[rows, lanes] = jnp.where(value_side, 0.0, dq).astype(BF16)
                slot_grad = dot_rows(
                    jnp.concatenate([score_grad, low], 0), jnp.concatenate([q, grad], 0)
                )
                for s in range(8):
                    where = slots_ref[base + s]
                    acc[where, :, lanes] += slot_grad[s * BLOCK : (s + 1) * BLOCK]

        @pl.when(step == blocks // STEP - 1)
        def _():
            def finish(i, _):
                own_ref[i] = acc[i]
                next_ref[i] = acc[blocks + i].astype(BF16)
                prev_ref[i] = acc[2 * blocks + i].astype(BF16)
                return _

            lax.fori_loop(0, blocks, finish, 0)
            glob_ref[...] = acc[3 * blocks :]

    shape = (blocks, BLOCK, heads * LANES)
    return pl.pallas_call(
        kernel,
        out_shape=(
            jax.ShapeDtypeStruct((blocks * BLOCK, heads * LANES), BF16),
            jax.ShapeDtypeStruct(shape, F32),
            jax.ShapeDtypeStruct(shape, BF16),
            jax.ShapeDtypeStruct(shape, BF16),
            jax.ShapeDtypeStruct((2,) + shape[1:], F32),
        ),
        grid_spec=pltpu.PrefetchScalarGridSpec(
            num_scalar_prefetch=1,
            grid=(blocks // STEP,),
            in_specs=[
                pl.BlockSpec((STEP * BLOCK, heads * LANES), lambda i, *_: (i, 0)),
                pl.BlockSpec((STEP, heads, BLOCK, 8 * BLOCK), lambda i, *_: (i, 0, 0, 0)),
                pl.BlockSpec((STEP * BLOCK, 2 * LANES), lambda i, *_: (i, 0)),
            ]
            + [pl.BlockSpec(memory_space=pl.ANY)] * many,
            out_specs=[
                pl.BlockSpec((STEP * BLOCK, heads * LANES), lambda i, *_: (i, 0)),
                pl.BlockSpec(shape, lambda i, *_: (0, 0, 0)),
                pl.BlockSpec(shape, lambda i, *_: (0, 0, 0)),
                pl.BlockSpec(shape, lambda i, *_: (0, 0, 0)),
                pl.BlockSpec((2,) + shape[1:], lambda i, *_: (0, 0, 0)),
            ],
            scratch_shapes=[
                pltpu.VMEM((3 * blocks + 2,) + shape[1:], BF16),
                pltpu.VMEM((3 * blocks + 2,) + shape[1:], F32),
                pltpu.SemaphoreType.DMA((many,)),
            ],
        ),
        compiler_params=pltpu.CompilerParams(vmem_limit_bytes=VMEM_LIMIT),
        cost_estimate=pl.CostEstimate(
            flops=40_000_000_000, bytes_accessed=30_000_000, transcendentals=0
        ),
        name="attend_backward",
    )(slots, queries, probs, context_grad, *pieces)


def norm_forward(value, gain, shift):
    center = value - jnp.mean(value, -1, keepdims=True)
    spread = jnp.mean(center * center, -1, keepdims=True)
    scale_row = lax.rsqrt(spread + NORM_EPS)
    normal = center * scale_row
    return (normal * gain + shift, normal, scale_row)


def norm_backward(grad, normal, scale_row, gain):
    gain_grad = jnp.sum(grad * normal, 0)
    shift_grad = jnp.sum(grad, 0)
    inner = grad * gain
    value_grad = scale_row * (
        inner
        - jnp.mean(inner, -1, keepdims=True)
        - normal * jnp.mean(inner * normal, -1, keepdims=True)
    )
    return (value_grad, gain_grad, shift_grad)


def slot_tables(place, global_blocks, random_blocks):
    ring = 2 * place.slabs
    half = 2 * place.n + place.c
    flip = 2 * place.x + place.h
    total = ring * 32
    found = []
    for j in range(2):
        arrived = place.to_heads(random_blocks, 0, j)
        arrived = lax.dynamic_slice_in_dim(arrived, 3 * place.x, 3, 0).reshape(3, 2, 8, 3)
        found.append(jnp.where(place.h == 0, arrived, arrived[:, ::-1]))
    chosen = jnp.concatenate(found, 1).reshape(3, 32, 3)
    order = jnp.arange(32, dtype=jnp.int32)
    query_ids = half * 32 + ((order // 8) ^ flip) * 8 + order % 8
    near = (query_ids[:, None] + jnp.arange(-1, 2, dtype=jnp.int32)) % total
    ids = jnp.concatenate(
        [
            jnp.broadcast_to(near[None], (3, 32, 3)),
            jnp.broadcast_to(global_blocks, (3, 32, 2)),
            chosen,
        ],
        -1,
    )
    earlier = jnp.arange(8)[None, :] < jnp.arange(8)[:, None]
    repeated = jnp.any((ids[..., :, None] == ids[..., None, :]) & earlier, -1)
    distance = (ids // 32 - half) % ring
    region = jnp.where(distance == 0, 0, jnp.where(distance == 1, 1, 2))
    within = ids % 32
    local = region * 32 + ((within // 8) ^ flip) * 8 + within % 8
    which = jnp.arange(8, dtype=jnp.int32)
    slots = jnp.where((which == 3) | (which == 4), 93 + which, local)
    marked = jnp.where(repeated, -1, ids)
    return slots.reshape(-1).astype(jnp.int32), marked.reshape(-1).astype(jnp.int32), query_ids.astype(jnp.int32)


def by_head(q, k, v):
    parts = [(m[..., :64], m[..., 64:128], m[..., 128:]) for m in (q, k, v)]
    (q0, q1, q2), (k0, k1, k2), (v0, v1, v2) = parts
    none = jnp.zeros_like(q0)
    return jnp.concatenate([none, q0, q1, none, none, q2, v0, k0, k1, v1, v2, k2], -1)


def from_head(value):
    parts = [value[..., 64 * i : 64 * i + 64] for i in range(12)]
    q = jnp.concatenate([parts[1], parts[2], parts[5]], -1)
    k = jnp.concatenate([parts[7], parts[8], parts[11]], -1)
    v = jnp.concatenate([parts[6], parts[9], parts[10]], -1)
    return q, k, v


def body(
    tokens,
    cotangent,
    doc_lengths,
    global_blocks,
    random_blocks,
    query_weight,
    query_bias,
    key_weight,
    value_weight,
    value_bias,
    output_weight,
    output_bias,
    first_gain,
    first_shift,
    up_weight,
    up_bias,
    down_weight,
    down_bias,
    second_gain,
    second_shift,
):
    place = Place()
    slabs = place.slabs
    devices = 8 * slabs
    tok_rows, width = tokens.shape
    share = query_weight.shape[0]
    hidden_width = up_weight.shape[1]
    scale = HEAD_DIM ** (-0.5)
    group = place.h * 2 + place.x
    flip = 2 * place.x + place.h
    order = ((0, 0), (1, 0), (0, 1), (1, 1))

    token_parts = [place.to_heads(tokens, i, j) for i, j in order]

    groups = by_head(
        (query_weight * BF16(scale)).reshape(share, 4, 192),
        key_weight.reshape(share, 4, 192),
        value_weight.reshape(share, 4, 192),
    ).transpose(1, 0, 2)
    vectors = jnp.concatenate(
        [query_bias, value_bias, output_bias, first_gain, first_shift, down_bias, second_gain, second_shift, up_bias]
    )
    vectors = jnp.pad(vectors, (0, width - vectors.shape[0]))
    groups = jnp.concatenate([groups, jnp.broadcast_to(vectors, (4, 1, width))], 1)
    arrived = gather_group(place, groups)
    w_heads = arrived[:, :share].reshape(width, width)
    rows = arrived[:, share]
    vec = rows[:, : 8 * share].reshape(devices, 8, share).transpose(1, 0, 2).reshape(8, width)
    vec = vec.astype(F32)
    b_query, b_value, b_output, gain_one, shift_one, b_down, gain_two, shift_two = (
        vec[i] for i in range(8)
    )
    b_up = rows[:, 8 * share : 12 * share].reshape(hidden_width).astype(F32)
    bq = pick(b_query.reshape(4, 192), group) * scale
    bv = pick(b_value.reshape(4, 192), group)
    b_heads = by_head(bq, jnp.zeros_like(bq), bv)

    owner = global_blocks // 8
    mine = owner == 2 * (4 * place.n + 2 * place.x + place.c) + place.h
    blocks_here = tokens.reshape(8, BLOCK, width)
    shown = jnp.stack(
        [jnp.where(mine[i], pick(blocks_here, global_blocks[i] % 8), 0) for i in range(2)]
    ).astype(BF16)
    total = shown
    for k in range(1, slabs):
        total = total + place.along_slabs(shown, k)
    shown = total
    for i, j in PAIRS[1:]:
        total = total + place.across(shown, i, j)
    global_tokens = (total + place.sibling(total)).reshape(2 * BLOCK, width)

    w_up = gather_shards(place, up_weight).reshape(width, hidden_width)
    w_down = gather_shards(place, down_weight).reshape(hidden_width, width)
    w_output = gather_shards(place, output_weight).reshape(width, width)

    query_parts, own, following, previous = [], [], [], []
    for part in token_parts:
        heads = (matmul(part, w_heads) + b_heads).astype(BF16)
        query_parts.append(heads[:, :384])
        kv = heads[:, 384:].reshape(8, BLOCK, 384)
        own.append(kv)
        following.append(place.to_previous(kv))
        previous.append(place.to_next(kv))
    shared = (matmul(global_tokens, w_heads[:, 384:]) + b_heads[384:]).astype(BF16)
    pieces = own + following + previous + [shared.reshape(2, BLOCK, 384)]
    queries = jnp.concatenate(query_parts, 0)

    which = jnp.arange(doc_lengths.shape[0])
    before = which[None, :] < which[:, None]
    starts = jnp.sum(jnp.where(before, doc_lengths[None, :], 0), 1).astype(jnp.int32)
    slots, ids, query_ids = slot_tables(place, global_blocks, random_blocks)
    context, probs = attend_forward(slots, ids, query_ids, starts, queries, pieces)

    context_tok = jnp.concatenate(
        [
            place.to_tokens(context[k * tok_rows : (k + 1) * tok_rows], i, j)
            for k, (i, j) in enumerate(order)
        ],
        1,
    )
    sources = [(place.h ^ i) * 2 + (place.c ^ j) for i, j in order]
    w_out = jnp.stack(
        [
            jnp.pad(pick(w_output.reshape(4, 192, width), source), ((0, 64), (0, 0)))
            for source in sources
        ]
    ).reshape(1024, width)

    first_sum = tokens.astype(F32) + matmul(context_tok, w_out) + b_output
    first, first_normal, first_scale = norm_forward(first_sum, gain_one, shift_one)
    first_low = first.astype(BF16)
    hidden = matmul(first_low, w_up) + b_up
    active, gelu_back = jax.vjp(partial(jax.nn.gelu, approximate=True), hidden)
    active_low = active.astype(BF16)
    second_sum = first + matmul(active_low, w_down) + b_down
    result, second_normal, second_scale = norm_forward(second_sum, gain_two, shift_two)
    second_grad, gain_two_grad, shift_two_grad = norm_backward(
        cotangent.astype(F32), second_normal, second_scale, gain_two
    )
    branch_grad = second_grad.astype(BF16)
    down_bias_grad = jnp.sum(branch_grad.astype(F32), 0)
    (hidden_grad,) = gelu_back(matmul(branch_grad, w_down.T))
    hidden_low = hidden_grad.astype(BF16)
    up_bias_grad = jnp.sum(hidden_low.astype(F32), 0)
    first_grad_in = second_grad + matmul(hidden_low, w_up.T)
    first_grad, gain_one_grad, shift_one_grad = norm_backward(
        first_grad_in, first_normal, first_scale, gain_one
    )
    attended_grad = first_grad.astype(BF16)
    output_bias_grad = jnp.sum(attended_grad.astype(F32), 0)
    context_grad = dot_lanes(attended_grad, w_out).astype(BF16)
    context_grad_parts = [
        place.to_heads(context_grad[:, 256 * k : 256 * k + 256], i, j)
        for k, (i, j) in enumerate(order)
    ]
    context_grad_rows = jnp.concatenate(context_grad_parts, 0)

    down_grad = dot_rows(active_low, branch_grad).astype(BF16)
    up_grad = dot_rows(first_low, hidden_low).astype(BF16)
    output_grad_parts = dot_rows(context_tok, attended_grad).astype(BF16).reshape(4, 256, width)[:, :192]
    output_grad_parts = jnp.stack(
        [output_grad_parts[0], output_grad_parts[2], output_grad_parts[1], output_grad_parts[3]]
    )
    token_group = place.h * 2 + place.c
    output_grad = jnp.stack([pick(output_grad_parts, token_group ^ g) for g in range(4)])
    chunked = (2, slabs, 2, 2)
    vector_grads = jnp.stack(
        [output_bias_grad, gain_one_grad, shift_one_grad, down_bias_grad, gain_two_grad, shift_two_grad]
    )
    vector_grads = vector_grads.reshape(6, devices, share).transpose(1, 0, 2).reshape(devices, 6 * share)
    vector_grads = jnp.concatenate([vector_grads, up_bias_grad.reshape(devices, 4 * share)], 1)
    vector_grads = jnp.pad(vector_grads, ((0, 0), (0, width - 10 * share))).astype(BF16)
    output_grad = jnp.concatenate(
        [output_grad.reshape(devices, share, width), vector_grads[:, None]], 1
    )
    down_share = scatter_sum(place, down_grad.reshape(chunked + (4 * share, width)))
    up_share = scatter_sum(place, up_grad.reshape(chunked + (share, hidden_width)))
    output_share = scatter_sum(place, output_grad.reshape(chunked + (share + 1, width)))

    query_grad, own_grad, next_grad, prev_grad, global_grad = attend_backward(
        slots, queries, probs, context_grad_rows, pieces
    )
    ring_sum = global_grad
    for k in range(1, slabs):
        ring_sum = ring_sum + place.along_slabs(global_grad, k)
    ring_sum = ring_sum + place.sibling(ring_sum)
    kv_grad = (
        own_grad + place.to_next(next_grad).astype(F32) + place.to_previous(prev_grad).astype(F32)
    )
    half = 2 * place.n + place.c
    for which in range(2):
        block = global_blocks[which]
        within = block % 32
        at = ((within // 8) ^ flip) * 8 + within % 8
        here = (jnp.arange(32) == at) & (block // 32 == half)
        kv_grad = kv_grad + jnp.where(here[:, None, None], ring_sum[which][None], 0.0)
    kv_grad = kv_grad.astype(BF16).reshape(2048, 384)
    heads_grad = jnp.concatenate([query_grad, kv_grad], 1)

    tokens_grad = first_grad
    for k, (i, j) in enumerate(order):
        part = dot_lanes(heads_grad[k * tok_rows : (k + 1) * tok_rows], w_heads).astype(BF16)
        tokens_grad = tokens_grad + place.to_tokens(part, i, j).astype(F32)

    token_rows = jnp.concatenate(token_parts, 0)
    heads_weight_grad = dot_rows(token_rows, heads_grad).astype(BF16)
    bias_grad = jnp.sum(heads_grad.astype(F32), 0).astype(BF16)
    chunks = jnp.concatenate(
        [
            heads_weight_grad.reshape(devices, share, width),
            jnp.broadcast_to(bias_grad, (devices, 1, width)),
        ],
        1,
    )
    found = scatter_group(place, chunks.reshape(chunked + (share + 1, width)))
    parts = [from_head(value) for value in found]
    query_all, key_all, value_all = (
        jnp.concatenate([part[i] for part in parts], -1) for i in range(3)
    )
    start = share * (place.h * 4 * slabs + 4 * place.n + 2 * place.x + place.c)
    query_all = query_all * scale
    query_bias_share = lax.dynamic_slice_in_dim(query_all[share], start, share)
    value_bias_share = lax.dynamic_slice_in_dim(value_all[share], start, share)
    small = output_share[share]
    pieces_of = [small[i * share : (i + 1) * share] for i in range(6)]

    return (
        result.astype(BF16),
        tokens_grad,
        query_all[:share],
        query_bias_share,
        key_all[:share],
        value_all[:share],
        value_bias_share,
        output_share[:share],
        pieces_of[0],
        pieces_of[1],
        pieces_of[2],
        up_share,
        small[6 * share : 10 * share],
        down_share,
        pieces_of[3],
        pieces_of[4],
        pieces_of[5],
    )


def solution(mesh):
    rows = P(("head", "blk"), None)
    vector = P(("head", "blk"))
    tokens = P(("blk", "head"), None)
    return jax.shard_map(
        body,
        mesh=mesh,
        in_specs=(
            tokens,
            tokens,
            P(),
            P(),
            P("head", "blk", None),
            rows,
            vector,
            rows,
            rows,
            vector,
            rows,
            vector,
            vector,
            vector,
            rows,
            vector,
            rows,
            vector,
            vector,
            vector,
        ),
        out_specs=(
            tokens,
            tokens,
            rows,
            vector,
            rows,
            rows,
            vector,
            rows,
            vector,
            vector,
            vector,
            rows,
            vector,
            rows,
            vector,
            vector,
            vector,
        ),
        check_vma=False,
    )
```

time: 1680 us -> 587 us (0.35)
  waiting for transfers between devices: 740 us -> 193 us
  local copies, waits for them, and re-layouts: 437 us -> 61.3 us
  matrix products: 225 us -> 58.8 us
  blocking collectives: 124 us -> 0 us
  Pallas kernels: 0 us -> 100 us
  starting transfers between devices: 54.7 us -> 124 us
  other arithmetic: 61.7 us -> 29.9 us
    reduce_scatter x3 -> x0, waiting for transfers between devices: 283 us -> none  [the longest x1 142 us: body(): lax.psum_scatter(every_grad[11], ('head', 'blk'), scatter_dimension=0, ti...]
    unnamed x17 -> x0, waiting for transfers between devices: 260 us -> none
    ppermute x8 -> x107, waiting for transfers between devices: 5.49 us -> 193 us  [send(): return lax.ppermute(value, AXES, route)]
    dot_general x34 -> x19, matrix products: 225 us -> 58.8 us  [the longest x10 38.5 us: matmul(): return jnp.dot(left, right, preferred_element_type=F32)]
    scatter x2 -> x0, local copies, waits for them, and re-layouts: 152 us -> none  [body(): slots = slots.at[:, :, 3 + which].set(spread_piece)]
    reshape x8, local copies, waits for them, and re-layouts: 132 us -> 2.26 us  [the longest x1 0.87 us: body(): value_weight.reshape(share, 4, 192)]
    all_gather x6 -> x0, waiting for transfers between devices: 115 us -> none  [the longest x1 53.5 us: body(): lax.all_gather(key_weight, ('head', 'blk'), axis=0, tiled=True)]
    pallas_call x0 -> x6, Pallas kernels: none -> 100 us  [the longest x1 40.4 us: attend_backward(): pl.pallas_call(kernel, out_shape=(jax.ShapeDtypeStruct((blocks * BLOCK, h...]
  transfers between devices with their start and end apart: 25 -> 107, of which waited for: 14 -> 37; matrix products, arithmetic and copies ran while one was open for 30% -> 17% of each run, Pallas kernels for 0% -> 17%
where the time goes in v1:
time: 587 us; the launch traced here: 576 us
  waiting for transfers between devices  193 us (33%)
  starting transfers between devices  124 us (21%)
  Pallas kernels  100 us (17%)
  local copies, waits for them, and re-layouts  61.3 us (10%)
  matrix products  58.8 us (10%)
  other arithmetic  29.9 us (5%)
  between operations  8.52 us (1%)
    ppermute x107, waiting for transfers between devices, send(): return lax.ppermute(value, AXES, route)  193 us
    ppermute x107, starting transfers between devices, send(): return lax.ppermute(value, AXES, route)  124 us
    pallas_call x1, Pallas kernels, attend_backward(): pl.pallas_call(kernel, out_shape=(jax.ShapeDtypeStruct((blocks * BLOCK, h...  40.4 us
    pallas_call x1, Pallas kernels, attend_forward(): pl.pallas_call(kernel, out_shape=(jax.ShapeDtypeStruct((blocks * BLOCK, 2...  40 us
    dot_general x10, matrix products, matmul(): return jnp.dot(left, right, preferred_element_type=F32)  38.5 us
    pallas_call x4, Pallas kernels, assemble(): pl.pallas_call(kernel, out_shape=jax.ShapeDtypeStruct((2, slabs, 2, 2, ro...  19.9 us
    dot_general x4, matrix products, dot_rows(): lax.dot_general(left, right, (((0,), (0,)), ((), ())), preferred_element_...  16 us
  transfers between devices with their start and end apart: 107, of which 37 were waited for; matrix products, arithmetic and copies ran while one was open for 17% of the time, Pallas kernels for 17%

profile of v1, /device:TPU:0, one launch (start us, length us, event | category | flops | bytes accessed | tf_op | source)
XLA Modules:
  0.0 575.6 jit_solution(16637027065148460188)
XLA Ops:
  0.7 5.1 collective-permute-start.57
  23.9 6.1 %concatenate.80 = bf16[288]{0:T(512)(128)(2,1)S(1)} concatenate(bf16[24]{0:T(256)(128)(2,1)} %param.26, bf16[24]{0:T(256)(128)(2,1)} %param.29, bf16[24]{0:T(256)(128)(2,1)} %param.31, bf16[24]{0:T(256)(128)(2,1)} %param.32, bf16[24]{0:T(256)(128)(2,1)} %param.33, bf16[24]{0:T(256)(128)(2,1)} %param.37, bf16[24]{0:T(256)(128)(2,1)} %param.38, bf16[24]{0:T(256)(128)(2,1)} %param.39, ...), dimensions={0} | concatenate | bytes 1152 | tf_op jit(solution)/shard_map/concatenate | solution.py:491
  45.9 5.2 collective-permute-start.2
  51.1 10.8 %collective-permute-done.46 = bf16[24,3072]{1,0:T(8,128)(2,1)S(1)} collective-permute-done((bf16[24,3072]{1,0:T(8,128)(2,1)S(1)}, bf16[24,3072]{1,0:T(8,128)(2,1)S(1)}, u32[]{:S(2)}, u32[]{:S(2)}) %collective-permute-start.46) | collective-permute-done | bytes 147488 | tf_op jit(solution)/shard_map/ppermute | solution.py:55
  63.6 8.6 %collective-permute-done.55 = bf16[96,768]{1,0:T(8,128)(2,1)S(1)} collective-permute-done((bf16[96,768]{1,0:T(8,128)(2,1)S(1)}, bf16[96,768]{1,0:T(8,128)(2,1)S(1)}, u32[]{:S(2)}, u32[]{:S(2)}) %collective-permute-start.55) | collective-permute-done | bytes 147488 | tf_op jit(solution)/shard_map/ppermute | solution.py:55
  109.8 7.4 %collective-permute-start.12 = (bf16[512,768]{1,0:T(8,128)(2,1)}, bf16[512,768]{1,0:T(8,128)(2,1)}, u32[]{:S(2)}, u32[]{:S(2)}) collective-permute-start(bf16[512,768]{1,0:T(8,128)(2,1)} %param.20), channel_id=1, source_target_pairs={{0,0},{1,2},{2,1},{3,3},{4,4},{5,6},{6,5},{7,7},{8,8},{9,10},{10,9... | collective-permute-start | bytes 2359304 | tf_op jit(solution)/shard_map/ppermute | solution.py:55
  143.6 13.4 %collective-permute-done.58.refs_1_ = bf16[4,96,768]{2,1,0:T(8,128)(2,1)} collective-permute-done((bf16[4,96,768]{2,1,0:T(8,128)(2,1)S(1)}, bf16[4,96,768]{2,1,0:T(8,128)(2,1)}, u32[]{:S(2)}, u32[]{:S(2)}) %collective-permute-start.58) | collective-permute-done | bytes 589856 | tf_op jit(solution)/shard_map/ppermute | solution.py:55
  160.3 9.5 %collective-permute-done.60.refs_3_ = bf16[4,96,768]{2,1,0:T(8,128)(2,1)} collective-permute-done((bf16[4,96,768]{2,1,0:T(8,128)(2,1)S(1)}, bf16[4,96,768]{2,1,0:T(8,128)(2,1)}, u32[]{:S(2)}, u32[]{:S(2)}) %collective-permute-start.60) | collective-permute-done | bytes 589856 | tf_op jit(solution)/shard_map/ppermute | solution.py:55
  170.7 11.7 %collective-permute-done.48.refs_1_ = bf16[4,24,3072]{2,1,0:T(8,128)(2,1)} collective-permute-done((bf16[4,24,3072]{2,1,0:T(8,128)(2,1)S(1)}, bf16[4,24,3072]{2,1,0:T(8,128)(2,1)}, u32[]{:S(2)}, u32[]{:S(2)}) %collective-permute-start.48) | collective-permute-done | bytes 589856 | tf_op jit(solution)/shard_map/ppermute | solution.py:55
  203.0 6.0 %collective-permute-done.19.refs_7_ = bf16[8,64,384]{2,1,0:T(8,128)(2,1)S(1)} collective-permute-done((bf16[8,64,384]{2,1,0:T(8,128)(2,1)S(1)}, bf16[8,64,384]{2,1,0:T(8,128)(2,1)S(1)}, u32[]{:S(2)}, u32[]{:S(2)}) %collective-permute-start.19) | collective-permute-done | bytes 393248 | tf_op jit(solution)/shard_map/ppermute | solution.py:55
  216.7 40.0 %attend_forward.1 = (bf16[2048,256]{1,0:T(8,128)(2,1)}, bf16[32,3,64,512]{3,2,1,0:T(8,128)(2,1)}) custom-call(s32[768]{0:T(1024)} %get-tuple-element.159.slots_ref, s32[768]{0:T(1024)} %get-tuple-element.158.ids_ref, s32[32]{0:T(128)} %copy-done.41, s32[8]{0:T(128)} %select_reduce_fusion.starts_ref, bf16[2048,384]{1,0:T(8,128)(2,1)} %pad_maximum_fusion.2.q_ref, ...), custom_call_target="tpu_custom_call" | custom-call | flops 20000000000 | bytes 20000000 | tf_op jit(solution)/shard_map/attend_forward/pallas_call | solution.py:255
  268.5 5.9 %assemble.7 = bf16[2,4,2,2,96,768]{5,4,3,2,1,0:T(8,128)(2,1)} custom-call(s32[4]{0:T(128)} %pad_add_fusion.2.where_ref, bf16[4,96,768]{2,1,0:T(8,128)(2,1)} %copy-done.7, bf16[4,96,768]{2,1,0:T(8,128)(2,1)} %collective-permute-done.58.refs_1_, bf16[4,96,768]{2,1,0:T(8,128)(2,1)} %collective-permute-done.59.refs_2_, ...), custom_call_target="tpu_custom_call" | custom-call | tf_op jit(solution)/shard_map/assemble/pallas_call | solution.py:101
  275.6 5.8 %assemble.6 = bf16[2,4,2,2,24,3072]{5,4,3,2,1,0:T(8,128)(2,1)} custom-call(s32[4]{0:T(128)} %pad_add_fusion.2.where_ref, bf16[4,24,3072]{2,1,0:T(8,128)(2,1)} %copy-done.6, bf16[4,24,3072]{2,1,0:T(8,128)(2,1)} %collective-permute-done.48.refs_1_, bf16[4,24,3072]{2,1,0:T(8,128)(2,1)} %collective-permute-done.49.refs_2_, ...), custom_call_target="tpu_custom_call" | custom-call | tf_op jit(solution)/shard_map/assemble/pallas_call | solution.py:101
  295.6 17.4 %fusion.133 = (bf16[3072]{0:T(1024)(128)(2,1)S(1)}, bf16[512,3072]{1,0:T(8,128)(2,1)S(1)}) fusion(f32[512,3072]{1,0:T(8,128)S(1)} %fusion.105, f32[3072]{0:T(1024)S(1)} %reshape.386, bf16[3072,768]{1,0:T(8,128)(2,1)S(1)} %bitcast.300, f32[512,768]{1,0:T(8,128)S(1)} %get-tuple-element.53), kind=kOutput, calls=%fused_computation.347 | convolution fusion | flops 2450912256 | bytes 15747072 | tf_op jit(solution)/shard_map/dot_general | solution.py:23
  323.7 5.7 convolution_convert_fusion
  347.0 40.4 %attend_backward.1 = (bf16[2048,384]{1,0:T(8,128)(2,1)}, f32[32,64,384]{2,1,0:T(8,128)}, bf16[32,64,384]{2,1,0:T(8,128)(2,1)}, bf16[32,64,384]{2,1,0:T(8,128)(2,1)}, f32[2,64,384]{2,1,0:T(8,128)}) custom-call(s32[768]{0:T(1024)} %get-tuple-element.159.slots_ref, bf16[2048,384]{1,0:T(8,128)(2,1)} %pad_maximum_fusion.2.q_ref, ...), custom_call_target="tpu_custom_call" | custom-call | flops 40000000000 | bytes 30000000 | tf_op jit(solution)/shard_map/attend_backward/pallas_call | solution.py:343
  397.4 15.2 %collective-permute-done.72 = f32[2,64,384]{2,1,0:T(8,128)S(1)} collective-permute-done((f32[2,64,384]{2,1,0:T(8,128)}, f32[2,64,384]{2,1,0:T(8,128)S(1)}, u32[]{:S(2)}, u32[]{:S(2)}) %collective-permute-start.72) | collective-permute-done | bytes 196640 | tf_op jit(solution)/shard_map/ppermute | solution.py:55
  426.5 7.0 %collective-permute-start.92 = (bf16[25,768]{1,0:T(8,128)(2,1)S(1)}, bf16[25,768]{1,0:T(8,128)(2,1)S(1)}, u32[]{:S(2)}, u32[]{:S(2)}) collective-permute-start(bf16[25,768]{1,0:T(8,128)(2,1)S(1)} %get-tuple-element.119), channel_id=1, source_target_pairs={{0,12},{1,13},{2,14},{3,15},{4,8},{5,9},{6,10},{7,11},{8,4},{9,5},... | collective-permute-start | bytes 115208 | tf_op jit(solution)/shard_map/ppermute | solution.py:55
  434.1 6.4 %collective-permute-done.92 = bf16[25,768]{1,0:T(8,128)(2,1)S(1)} collective-permute-done((bf16[25,768]{1,0:T(8,128)(2,1)S(1)}, bf16[25,768]{1,0:T(8,128)(2,1)S(1)}, u32[]{:S(2)}, u32[]{:S(2)}) %collective-permute-start.92) | collective-permute-done | bytes 38432 | tf_op jit(solution)/shard_map/ppermute | solution.py:55
  441.0 6.2 %collective-permute-done.91 = bf16[25,768]{1,0:T(8,128)(2,1)S(1)} collective-permute-done((bf16[25,768]{1,0:T(8,128)(2,1)S(1)}, bf16[25,768]{1,0:T(8,128)(2,1)S(1)}, u32[]{:S(2)}, u32[]{:S(2)}) %collective-permute-start.91) | collective-permute-done | bytes 38432 | tf_op jit(solution)/shard_map/ppermute | solution.py:55
  479.1 6.5 %collective-permute-done.81 = bf16[2,2,25,768]{3,1,2,0:T(2,128)(2,1)S(1)} collective-permute-done((bf16[2,2,25,768]{3,1,2,0:T(2,128)(2,1)S(1)}, bf16[2,2,25,768]{3,1,2,0:T(2,128)(2,1)S(1)}, u32[]{:S(2)}, u32[]{:S(2)}) %collective-permute-start.81) | collective-permute-done | bytes 153632 | tf_op jit(solution)/shard_map/ppermute | solution.py:55
  499.0 22.4 %collective-permute-done.85 = f32[25,768]{1,0:T(8,128)S(1)} collective-permute-done((f32[25,768]{1,0:T(8,128)S(1)}, f32[25,768]{1,0:T(8,128)S(1)}, u32[]{:S(2)}, u32[]{:S(2)}) %collective-permute-start.85) | collective-permute-done | bytes 76832 | tf_op jit(solution)/shard_map/ppermute | solution.py:55
  553.7 5.1 collective-permute-done.101
  568.9 5.5 collective-permute-done.105
  (547 shorter events, 293.7 us)
Async XLA Ops:
  0.7 41.8 %collective-permute-start.57 = (bf16[96,768]{1,0:T(8,128)(2,1)}, bf16[96,768]{1,0:T(8,128)(2,1)S(1)}, u32[]{:S(2)}, u32[]{:S(2)}) collective-permute-start(bf16[96,768]{1,0:T(8,128)(2,1)} %param.36), channel_id=1, source_target_pairs={{0,12},{1,13},{2,14},{3,15},{4,8},{5,9},{6,10},{7,11},{8,4},{9,5},... | collective-permute-start | bytes 442376 | tf_op jit(solution)/shard_map/ppermute | solution.py:55
  5.8 38.6 %collective-permute-start.56 = (bf16[96,768]{1,0:T(8,128)(2,1)}, bf16[96,768]{1,0:T(8,128)(2,1)S(1)}, u32[]{:S(2)}, u32[]{:S(2)}) collective-permute-start(bf16[96,768]{1,0:T(8,128)(2,1)} %param.36), channel_id=1, source_target_pairs={{0,8},{1,9},{2,10},{3,11},{4,12},{5,13},{6,14},{7,15},{8,0},{9,1},... | collective-permute-start | bytes 442376 | tf_op jit(solution)/shard_map/ppermute | solution.py:55
  42.5 33.0 %collective-permute-start.4 = (bf16[4,25,768]{2,1,0:T(8,128)(2,1)S(1)}, bf16[4,25,768]{2,1,0:T(8,128)(2,1)S(1)}, u32[]{:S(2)}, u32[]{:S(2)}) collective-permute-start(bf16[4,25,768]{2,1,0:T(8,128)(2,1)S(1)} %get-tuple-element.124), channel_id=1, source_target_pairs={{0,12},{1,13},{2,14},{3,15},{4,8},{5,9},{6,10},{7,11},{8,4},{9,5},... | collective-permute-start | bytes 460808 | tf_op jit(solution)/shard_map/ppermute | solution.py:55
  44.3 31.3 %collective-permute-start.3 = (bf16[4,25,768]{2,1,0:T(8,128)(2,1)S(1)}, bf16[4,25,768]{2,1,0:T(8,128)(2,1)S(1)}, u32[]{:S(2)}, u32[]{:S(2)}) collective-permute-start(bf16[4,25,768]{2,1,0:T(8,128)(2,1)S(1)} %get-tuple-element.124), channel_id=1, source_target_pairs={{0,8},{1,9},{2,10},{3,11},{4,12},{5,13},{6,14},{7,15},{8,0},{9,1},... | collective-permute-start | bytes 460808 | tf_op jit(solution)/shard_map/ppermute | solution.py:55
  45.9 30.8 %collective-permute-start.2 = (bf16[4,25,768]{2,1,0:T(8,128)(2,1)S(1)}, bf16[4,25,768]{2,1,0:T(8,128)(2,1)S(1)}, u32[]{:S(2)}, u32[]{:S(2)}) collective-permute-start(bf16[4,25,768]{2,1,0:T(8,128)(2,1)S(1)} %get-tuple-element.124), channel_id=1, source_target_pairs={{0,4},{1,5},{2,6},{3,7},{4,0},{5,1},{6,2},{7,3},{8,12},{9,13},{10,... | collective-permute-start | bytes 460808 | tf_op jit(solution)/shard_map/ppermute | solution.py:55
  100.0 84.5 %collective-permute-start.15 = (bf16[512,768]{1,0:T(8,128)(2,1)}, bf16[512,768]{1,0:T(8,128)(2,1)}, u32[]{:S(2)}, u32[]{:S(2)}) collective-permute-start(bf16[512,768]{1,0:T(8,128)(2,1)} %param.20), channel_id=1, source_target_pairs={{0,18},{1,16},{2,19},{3,17},{4,22},{5,20},{6,23},{7,21},{8,26},{9,... | collective-permute-start | bytes 2359304 | tf_op jit(solution)/shard_map/ppermute | solution.py:55
  108.7 32.8 %collective-permute-start.13 = (bf16[512,768]{1,0:T(8,128)(2,1)}, bf16[512,768]{1,0:T(8,128)(2,1)}, u32[]{:S(2)}, u32[]{:S(2)}) collective-permute-start(bf16[512,768]{1,0:T(8,128)(2,1)} %param.20), channel_id=1, source_target_pairs={{0,16},{1,18},{2,17},{3,19},{4,20},{5,22},{6,21},{7,23},{8,24},{9,... | collective-permute-start | bytes 2359304 | tf_op jit(solution)/shard_map/ppermute | solution.py:55
  109.8 47.2 %collective-permute-start.12 = (bf16[512,768]{1,0:T(8,128)(2,1)}, bf16[512,768]{1,0:T(8,128)(2,1)}, u32[]{:S(2)}, u32[]{:S(2)}) collective-permute-start(bf16[512,768]{1,0:T(8,128)(2,1)} %param.20), channel_id=1, source_target_pairs={{0,0},{1,2},{2,1},{3,3},{4,4},{5,6},{6,5},{7,7},{8,8},{9,10},{10,9... | collective-permute-start | bytes 2359304 | tf_op jit(solution)/shard_map/ppermute | solution.py:55
  126.6 30.5 %collective-permute-start.58 = (bf16[4,96,768]{2,1,0:T(8,128)(2,1)S(1)}, bf16[4,96,768]{2,1,0:T(8,128)(2,1)}, u32[]{:S(2)}, u32[]{:S(2)}) collective-permute-start(bf16[4,96,768]{2,1,0:T(8,128)(2,1)S(1)} %pad_maximum_fusion.11.refs_0_), channel_id=1, source_target_pairs={{0,16},{1,17},{2,18},{3,19},{4,20},{5,21},{6,22},{7,23},{8,24},{9,... | collective-permute-start | bytes 1769480 | tf_op jit(solution)/shard_map/ppermute | solution.py:55
  209.0 47.7 %collective-permute-start.51 = (bf16[4,24,3072]{2,1,0:T(8,128)(2,1)S(1)}, bf16[4,24,3072]{2,1,0:T(8,128)(2,1)S(1)}, u32[]{:S(2)}, u32[]{:S(2)}) collective-permute-start(bf16[4,24,3072]{2,1,0:T(8,128)(2,1)S(1)} %pad_maximum_fusion.10.refs_0_), channel_id=1, source_target_pairs={{0,1},{1,0},{2,3},{3,2},{4,5},{5,4},{6,7},{7,6},{8,9},{9,8},{10,11... | collective-permute-start | bytes 1769480 | tf_op jit(solution)/shard_map/ppermute | solution.py:55
  209.0 47.8 %collective-permute-start.62 = (bf16[4,96,768]{2,1,0:T(8,128)(2,1)}, bf16[4,96,768]{2,1,0:T(8,128)(2,1)}, u32[]{:S(2)}, u32[]{:S(2)}) collective-permute-start(bf16[4,96,768]{2,1,0:T(8,128)(2,1)} %collective-permute-done.58.refs_1_), channel_id=1, source_target_pairs={{0,1},{1,0},{2,3},{3,2},{4,5},{5,4},{6,7},{7,6},{8,9},{9,8},{10,11... | collective-permute-start | bytes 1769480 | tf_op jit(solution)/shard_map/ppermute | solution.py:55
  209.5 50.0 %collective-permute-start.63 = (bf16[4,96,768]{2,1,0:T(8,128)(2,1)}, bf16[4,96,768]{2,1,0:T(8,128)(2,1)}, u32[]{:S(2)}, u32[]{:S(2)}) collective-permute-start(bf16[4,96,768]{2,1,0:T(8,128)(2,1)} %collective-permute-done.59.refs_2_), channel_id=1, source_target_pairs={{0,1},{1,0},{2,3},{3,2},{4,5},{5,4},{6,7},{7,6},{8,9},{9,8},{10,11... | collective-permute-start | bytes 1769480 | tf_op jit(solution)/shard_map/ppermute | solution.py:55
  211.8 51.5 %collective-permute-start.64 = (bf16[4,96,768]{2,1,0:T(8,128)(2,1)}, bf16[4,96,768]{2,1,0:T(8,128)(2,1)}, u32[]{:S(2)}, u32[]{:S(2)}) collective-permute-start(bf16[4,96,768]{2,1,0:T(8,128)(2,1)} %collective-permute-done.60.refs_3_), channel_id=1, source_target_pairs={{0,1},{1,0},{2,3},{3,2},{4,5},{5,4},{6,7},{7,6},{8,9},{9,8},{10,11... | collective-permute-start | bytes 1769480 | tf_op jit(solution)/shard_map/ppermute | solution.py:55
  216.0 47.5 %collective-permute-start.52 = (bf16[4,24,3072]{2,1,0:T(8,128)(2,1)}, bf16[4,24,3072]{2,1,0:T(8,128)(2,1)}, u32[]{:S(2)}, u32[]{:S(2)}) collective-permute-start(bf16[4,24,3072]{2,1,0:T(8,128)(2,1)} %collective-permute-done.48.refs_1_), channel_id=1, source_target_pairs={{0,1},{1,0},{2,3},{3,2},{4,5},{5,4},{6,7},{7,6},{8,9},{9,8},{10,11... | collective-permute-start | bytes 1769480 | tf_op jit(solution)/shard_map/ppermute | solution.py:55
  339.1 74.0 %collective-permute-start.86 = (bf16[2,4,2,25,768]{4,1,3,2,0:T(4,128)(2,1)}, bf16[2,4,2,25,768]{4,1,3,2,0:T(4,128)(2,1)S(1)}, u32[]{:S(2)}, u32[]{:S(2)}) collective-permute-start(bf16[2,4,2,25,768]{4,1,3,2,0:T(4,128)(2,1)} %copy.208), channel_id=1, source_target_pairs={{0,1},{1,0},{2,3},{3,2},{4,5},{5,4},{6,7},{7,6},{8,9},{9,8},{10,11... | collective-permute-start | bytes 1843208 | tf_op jit(solution)/shard_map/ppermute | solution.py:55
  394.0 55.1 %collective-permute-start.70 = (bf16[32,64,384]{2,1,0:T(8,128)(2,1)S(1)}, bf16[32,64,384]{2,1,0:T(8,128)(2,1)S(1)}, u32[]{:S(2)}, u32[]{:S(2)}) collective-permute-start(bf16[32,64,384]{2,1,0:T(8,128)(2,1)S(1)} %copy-done.43), channel_id=1, source_target_pairs={{0,13},{1,0},{2,15},{3,2},{4,1},{5,4},{6,3},{7,6},{8,5},{9,8},{10,... | collective-permute-start | bytes 4718600 | tf_op jit(solution)/shard_map/ppermute | solution.py:55
  397.4 51.7 %collective-permute-start.69 = (bf16[32,64,384]{2,1,0:T(8,128)(2,1)S(1)}, bf16[32,64,384]{2,1,0:T(8,128)(2,1)S(1)}, u32[]{:S(2)}, u32[]{:S(2)}) collective-permute-start(bf16[32,64,384]{2,1,0:T(8,128)(2,1)S(1)} %copy-done.42), channel_id=1, source_target_pairs={{0,1},{1,4},{2,3},{3,6},{4,5},{5,8},{6,7},{7,10},{8,9},{9,12},{10,... | collective-permute-start | bytes 4718600 | tf_op jit(solution)/shard_map/ppermute | solution.py:55
  451.4 41.2 %collective-permute-start.78 = (bf16[512,768]{1,0:T(8,128)(2,1)S(1)}, bf16[512,768]{1,0:T(8,128)(2,1)S(1)}, u32[]{:S(2)}, u32[]{:S(2)}) collective-permute-start(bf16[512,768]{1,0:T(8,128)(2,1)S(1)} %convolution_convert_fusion.4), channel_id=1, source_target_pairs={{0,17},{1,19},{2,16},{3,18},{4,21},{5,23},{6,20},{7,22},{8,25},{9,... | collective-permute-start | bytes 2359304 | tf_op jit(solution)/shard_map/ppermute | solution.py:55
  453.4 40.6 %collective-permute-start.77 = (bf16[512,768]{1,0:T(8,128)(2,1)S(1)}, bf16[512,768]{1,0:T(8,128)(2,1)S(1)}, u32[]{:S(2)}, u32[]{:S(2)}) collective-permute-start(bf16[512,768]{1,0:T(8,128)(2,1)S(1)} %convolution_convert_fusion.5), channel_id=1, source_target_pairs={{0,1},{1,3},{2,0},{3,2},{4,5},{5,7},{6,4},{7,6},{8,9},{9,11},{10,8... | collective-permute-start | bytes 2359304 | tf_op jit(solution)/shard_map/ppermute | solution.py:55
  455.3 40.5 %collective-permute-start.76 = (bf16[512,768]{1,0:T(8,128)(2,1)S(1)}, bf16[512,768]{1,0:T(8,128)(2,1)S(1)}, u32[]{:S(2)}, u32[]{:S(2)}) collective-permute-start(bf16[512,768]{1,0:T(8,128)(2,1)S(1)} %convolution_convert_fusion.6), channel_id=1, source_target_pairs={{0,16},{1,18},{2,17},{3,19},{4,20},{5,22},{6,21},{7,23},{8,24},{9,... | collective-permute-start | bytes 2359304 | tf_op jit(solution)/shard_map/ppermute | solution.py:55
  490.8 54.2 %collective-permute-start.96 = (bf16[4,24,3072]{2,1,0:T(8,128)(2,1)}, bf16[4,24,3072]{2,1,0:T(8,128)(2,1)S(1)}, u32[]{:S(2)}, u32[]{:S(2)}) collective-permute-start(bf16[4,24,3072]{2,1,0:T(8,128)(2,1)} %get-tuple-element.60), channel_id=1, source_target_pairs={{0,18},{1,19},{2,16},{3,17},{4,22},{5,23},{6,20},{7,21},{8,26},{9,... | collective-permute-start | bytes 1769480 | tf_op jit(solution)/shard_map/ppermute | solution.py:55
  492.6 52.9 %collective-permute-start.95 = (bf16[4,24,3072]{2,1,0:T(8,128)(2,1)}, bf16[4,24,3072]{2,1,0:T(8,128)(2,1)S(1)}, u32[]{:S(2)}, u32[]{:S(2)}) collective-permute-start(bf16[4,24,3072]{2,1,0:T(8,128)(2,1)} %get-tuple-element.61), channel_id=1, source_target_pairs={{0,2},{1,3},{2,0},{3,1},{4,6},{5,7},{6,4},{7,5},{8,10},{9,11},{10,... | collective-permute-start | bytes 1769480 | tf_op jit(solution)/shard_map/ppermute | solution.py:55
  521.9 29.0 %collective-permute-start.103 = (bf16[4,96,768]{2,1,0:T(8,128)(2,1)}, bf16[4,96,768]{2,1,0:T(8,128)(2,1)}, u32[]{:S(2)}, u32[]{:S(2)}) collective-permute-start(bf16[4,96,768]{2,1,0:T(8,128)(2,1)} %get-tuple-element.57), channel_id=1, source_target_pairs={{0,18},{1,19},{2,16},{3,17},{4,22},{5,23},{6,20},{7,21},{8,26},{9,... | collective-permute-start | bytes 1769480 | tf_op jit(solution)/shard_map/ppermute | solution.py:55
  523.9 29.8 %collective-permute-start.102 = (bf16[4,96,768]{2,1,0:T(8,128)(2,1)}, bf16[4,96,768]{2,1,0:T(8,128)(2,1)}, u32[]{:S(2)}, u32[]{:S(2)}) collective-permute-start(bf16[4,96,768]{2,1,0:T(8,128)(2,1)} %get-tuple-element.58), channel_id=1, source_target_pairs={{0,2},{1,3},{2,0},{3,1},{4,6},{5,7},{6,4},{7,5},{8,10},{9,11},{10,... | collective-permute-start | bytes 1769480 | tf_op jit(solution)/shard_map/ppermute | solution.py:55
  (143 other events, 2133.5 us)

commit v2 on v1

v2 whole, which is shorter than its diff:
```python
from functools import partial

import jax
import jax.numpy as jnp
from jax import lax
from jax.experimental import pallas as pl
from jax.experimental.pallas import tpu as pltpu
from jax.sharding import Mesh
from jax.sharding import PartitionSpec as P

HEAD_DIM = 64
BLOCK = 64
LANES = 128
NORM_EPS = 1e-06
MASKED = -1e30
AXES = ("head", "slab", "x", "core")
CHIPS = ("head", "x")
BF16 = jnp.bfloat16
F32 = jnp.float32
PAIRS = ((0, 0), (0, 1), (1, 0), (1, 1))
VMEM_LIMIT = 60 * 1024 * 1024


def matmul(left, right):
    return jnp.dot(left, right, preferred_element_type=F32)


def dot_rows(left, right):
    return lax.dot_general(left, right, (((0,), (0,)), ((), ())), preferred_element_type=F32)


def dot_lanes(left, right):
    return lax.dot_general(left, right, (((1,), (1,)), ((), ())), preferred_element_type=F32)


class Place:
    def __init__(self):
        self.slabs = lax.axis_size("slab")
        self.size = 4 * self.slabs
        self.h, self.n, self.x, self.c = (lax.axis_index(axis) for axis in AXES)

    def send(self, value, target):
        def index(h, n, x, c):
            return h * self.size + 4 * n + 2 * x + c

        route = [
            (index(h, n, x, c), index(*target(h, n, x, c)))
            for h in range(2)
            for n in range(self.slabs)
            for x in range(2)
            for c in range(2)
        ]
        return lax.ppermute(value, AXES, route)

    def along_slabs(self, value, k):
        return self.send(value, lambda h, n, x, c: (h, n ^ k, x, c))

    def across(self, value, i, j):
        return self.send(value, lambda h, n, x, c: (h ^ i, n, x ^ j, c))

    def sibling(self, value):
        return self.send(value, lambda h, n, x, c: (h, n, x, 1 - c))

    def to_heads(self, value, i, j):
        return self.send(value, lambda h, n, x, c: (h ^ i, n, c ^ j, x))

    def to_tokens(self, value, i, j):
        return self.send(value, lambda h, n, x, c: (h ^ i, n, c, x ^ j))

    def to_next(self, value):
        def target(h, n, x, c):
            return (h, n, x, 1) if c == 0 else (h, (n + 1) % self.slabs, x, 0)

        return self.send(value, target)

    def to_previous(self, value):
        def target(h, n, x, c):
            return (h, n, x, 0) if c == 1 else (h, (n - 1) % self.slabs, x, 1)

        return self.send(value, target)


def exchange(value, axes):
    return lax.all_to_all(value, axes, split_axis=0, concat_axis=0, tiled=True)


def pick(value, index, axis=0):
    return lax.dynamic_index_in_dim(value, index, axis, keepdims=False)


def kernel_call(kernel, out_shape, name, flops=1000, **options):
    return pl.pallas_call(
        kernel,
        out_shape=out_shape,
        compiler_params=pltpu.CompilerParams(vmem_limit_bytes=VMEM_LIMIT),
        cost_estimate=pl.CostEstimate(
            flops=flops, bytes_accessed=1000, transcendentals=0
        ),
        name=name,
        **options,
    )


def whole(count):
    return [pl.BlockSpec(memory_space=pltpu.VMEM)] * count


def smem():
    return pl.BlockSpec(memory_space=pltpu.SMEM)


def after(value, *others):
    return lax.optimization_barrier((value,) + others)[0]


def side_of(head):
    return 1 - head % 2


def half_tile(value, start, side):
    tile = start // LANES * LANES
    found = value[:, tile : tile + LANES].astype(F32)
    if (start % LANES) // HEAD_DIM != side:
        found = pltpu.roll(found, HEAD_DIM, 1)
    return found


def left_lanes(rows):
    return lax.broadcasted_iota(jnp.int32, (rows, LANES), 1) < HEAD_DIM


def pack_heads(query_weight, key_weight, value_weight, biases, scale):
    share = query_weight.shape[0]

    def kernel(q_ref, k_ref, v_ref, b_ref, out_ref):
        left = left_lanes(share)
        for group in range(4):
            start = 3 * group * HEAD_DIM
            q = [half_tile(q_ref, start + t * HEAD_DIM, side_of(t)) * scale for t in range(3)]
            out_ref[group, :, :LANES] = jnp.where(left, q[1], q[0]).astype(BF16)
            extra = b_ref[...].astype(F32)
            out_ref[group, :, LANES : 2 * LANES] = jnp.where(left, extra, q[2]).astype(BF16)
            for t in range(3):
                side = side_of(t)
                k = half_tile(k_ref, start + t * HEAD_DIM, side)
                v = half_tile(v_ref, start + t * HEAD_DIM, 1 - side)
                both = jnp.where(left, k, v) if side == 0 else jnp.where(left, v, k)
                out_ref[group, :, (2 + t) * LANES : (3 + t) * LANES] = both.astype(BF16)

    return kernel_call(
        kernel,
        jax.ShapeDtypeStruct((4, share, 5 * LANES), BF16),
        "pack_heads",
        in_specs=whole(4),
        out_specs=whole(1)[0],
    )(query_weight, key_weight, value_weight, biases)


def pack_rest(up, down, output, vectors):
    share, width = output.shape
    height = -(-(9 * share + 8) // 16) * 16
    count = len(vectors)

    def kernel(up_ref, down_ref, output_ref, *refs):
        out_ref = refs[-1]
        for i in range(4):
            out_ref[i * share : (i + 1) * share] = up_ref[:, i * width : (i + 1) * width]
        out_ref[4 * share : 8 * share] = down_ref[...]
        out_ref[8 * share : 9 * share] = output_ref[...]
        row = lax.broadcasted_iota(jnp.int32, (height - 9 * share, LANES), 0)
        total = jnp.zeros(row.shape, F32)
        for i, ref in enumerate(refs[:count]):
            total = jnp.where(row == i, jnp.broadcast_to(ref[...].astype(F32), row.shape), total)
        out_ref[9 * share :, :LANES] = total.astype(BF16)
        out_ref[9 * share :, LANES:] = jnp.zeros((height - 9 * share, width - LANES), BF16)

    vectors = [jnp.pad(v, (0, LANES - v.shape[0]))[None] for v in vectors]
    return kernel_call(
        kernel,
        jax.ShapeDtypeStruct((height, width), BF16),
        "pack_rest",
        in_specs=whole(3 + count),
        out_specs=whole(1)[0],
    )(up, down, output, *vectors)


def stack_heads(parts):
    def kernel(*refs):
        for k, ref in enumerate(refs[:-1]):
            refs[-1][k] = ref[...]

    return kernel_call(
        kernel,
        jax.ShapeDtypeStruct((len(parts),) + parts[0].shape, BF16),
        "stack_heads",
        in_specs=whole(len(parts)),
        out_specs=whole(1)[0],
    )(*parts)


def assemble_heads(place, column, other):
    slabs, _, rows, columns = column.shape
    where = jnp.stack([place.h, place.n, place.x, place.c]).astype(jnp.int32)

    def kernel(where_ref, mine_ref, other_ref, out_ref, bias_ref):
        h, x, c = where_ref[0], where_ref[2], where_ref[3]
        left = left_lanes(rows)
        right = jnp.logical_not(left)
        for core, ref in enumerate((mine_ref, other_ref)):
            for p, (i, j) in enumerate(PAIRS):
                first = ref[0, p, :, :LANES].astype(F32)
                second = ref[0, p, :, LANES : 2 * LANES]
                q = (
                    jnp.where(right, first, 0.0),
                    jnp.where(left, first, 0.0),
                    jnp.where(right, second.astype(F32), 0.0),
                )
                at = (h ^ i, 0, x ^ j, c ^ core)
                for t in range(3):
                    out_ref[(*at, slice(None), slice(t * LANES, (t + 1) * LANES))] = q[t].astype(BF16)
                out_ref[(*at, slice(None), slice(3 * LANES, 6 * LANES))] = ref[0, p, :, 2 * LANES :]
                bias_ref[at] = second

    found = kernel_call(
        kernel,
        (
            jax.ShapeDtypeStruct((2, slabs, 2, 2, rows, 6 * LANES), BF16),
            jax.ShapeDtypeStruct((2, slabs, 2, 2, rows, LANES), BF16),
        ),
        "assemble_heads",
        grid_spec=pltpu.PrefetchScalarGridSpec(
            num_scalar_prefetch=1,
            grid=(slabs,),
            in_specs=[pl.BlockSpec((1, 4, rows, columns), lambda k, w: (k, 0, 0, 0))] * 2,
            out_specs=[
                pl.BlockSpec((2, 1, 2, 2, rows, 6 * LANES), lambda k, w: (0, k ^ w[1], 0, 0, 0, 0)),
                pl.BlockSpec((2, 1, 2, 2, rows, LANES), lambda k, w: (0, k ^ w[1], 0, 0, 0, 0)),
            ],
        ),
    )(where, column, other)
    return [value.reshape(8 * slabs, *value.shape[4:]) for value in found]


def assemble_rest(place, mine, other, share):
    _, slabs, rows, width = mine.shape
    where = place.c.reshape(1).astype(jnp.int32)

    def kernel(where_ref, mine_ref, other_ref, up_ref, down_ref, output_ref, vector_ref):
        for core, ref in ((where_ref[0], mine_ref), (1 - where_ref[0], other_ref)):
            for p in range(4):
                at = (p // 2, 0, p % 2, core)
                for q in range(4):
                    columns = slice(q * width, (q + 1) * width)
                    up_ref[(*at, slice(None), columns)] = ref[p, 0, q * share : (q + 1) * share]
                down_ref[at] = ref[p, 0, 4 * share : 8 * share]
                output_ref[at] = ref[p, 0, 8 * share : 9 * share]
                vector_ref[at] = ref[p, 0, 9 * share :]

    shapes = ((share, 4 * width), (4 * share, width), (share, width), (rows - 9 * share, width))
    found = kernel_call(
        kernel,
        tuple(jax.ShapeDtypeStruct((2, slabs, 2, 2) + shape, BF16) for shape in shapes),
        "assemble_rest",
        grid_spec=pltpu.PrefetchScalarGridSpec(
            num_scalar_prefetch=1,
            grid=(slabs,),
            in_specs=[pl.BlockSpec((4, 1, rows, width), lambda n, w: (0, n, 0, 0))] * 2,
            out_specs=[
                pl.BlockSpec((2, 1, 2, 2) + shape, lambda n, w: (0, n, 0, 0, 0, 0)) for shape in shapes
            ],
        ),
    )(where, mine, other)
    return [value.reshape(8 * slabs, *value.shape[4:]) for value in found]


def weight_grads(place, active, branch_grad, first, hidden_grad, context, attended_grad, vectors):
    devices = 8 * place.slabs
    step = devices // 4
    tokens, width = first.shape
    share = width // devices
    rows = -(-(9 * share + 8) // 16) * 16
    where = jnp.stack([place.h * 2 + place.c, place.c]).astype(jnp.int32)

    def kernel(where_ref, active_ref, branch_ref, first_ref, hidden_ref, context_ref, attended_ref, vector_ref, kept_ref, sent_ref):
        even = where_ref[1] == 0

        def put(start, stop, value):
            value = value.astype(BF16).reshape(step, stop - start, width)
            for p in range(step // 2):
                kept_ref[p, start:stop] = jnp.where(even, value[2 * p], value[2 * p + 1])
                sent_ref[p, start:stop] = jnp.where(even, value[2 * p + 1], value[2 * p])

        put(4 * share, 8 * share, dot_rows(active_ref[...], branch_ref[...]))
        columns = first_ref[...]
        for q in range(4):
            up = dot_rows(columns, hidden_ref[:, q * width : (q + 1) * width])
            put(q * share, (q + 1) * share, up[: step * share])
        put(8 * share, 9 * share, dot_rows(context_ref[...], attended_ref[...])[: step * share])
        for p in range(step // 2):
            for ref, at in ((kept_ref, 2 * p + where_ref[1]), (sent_ref, 2 * p + 1 - where_ref[1])):
                ref[p, 9 * share :] = jnp.zeros((rows - 9 * share, width), BF16)
                ref[p, 9 * share : 9 * share + 8, :LANES] = vector_ref[at].astype(BF16)

    first = jnp.pad(first.reshape(tokens, 4, 192), ((0, 0), (0, 0), (0, 64))).reshape(tokens, 1024)
    half = jax.ShapeDtypeStruct((devices // 2, rows, width), BF16)
    return kernel_call(
        kernel,
        (half, half),
        "weight_grads",
        15_000_000_000,
        grid_spec=pltpu.PrefetchScalarGridSpec(
            num_scalar_prefetch=1,
            grid=(4,),
            in_specs=[
                pl.BlockSpec((tokens, width), lambda g, w: (0, g)),
                pl.BlockSpec((tokens, width), lambda g, w: (0, 0)),
                pl.BlockSpec((tokens, 256), lambda g, w: (0, g)),
                pl.BlockSpec((tokens, 4 * width), lambda g, w: (0, 0)),
                pl.BlockSpec((tokens, 256), lambda g, w: (0, g ^ w[0])),
                pl.BlockSpec((tokens, width), lambda g, w: (0, 0)),
                pl.BlockSpec((step, 8, LANES), lambda g, w: (g, 0, 0)),
            ],
            out_specs=[pl.BlockSpec((step // 2, rows, width), lambda g, w: (g, 0, 0))] * 2,
        ),
    )(where, active, branch_grad, first, hidden_grad, context, attended_grad, vectors)


def heads_weight_grads(place, token_rows, heads_grads, bias_grads):
    slabs = place.slabs
    width = token_rows[0].shape[1]
    share = width // (8 * slabs)
    rows = -(-(share + 1) // 16) * 16
    where = place.c.reshape(1).astype(jnp.int32)

    def kernel(where_ref, x0_ref, x1_ref, g0_ref, g1_ref, b0_ref, b1_ref, kept_ref, sent_ref):
        even = where_ref[0] == 0
        bias = jnp.broadcast_to(b0_ref[...] + b1_ref[...], (rows - share, width)).astype(BF16)
        value = dot_rows(x0_ref[...], g0_ref[...]) + dot_rows(x1_ref[...], g1_ref[...])
        value = value.astype(BF16).reshape(8 * slabs, share, width)
        for p in range(4 * slabs):
            kept_ref[p, :share] = jnp.where(even, value[2 * p], value[2 * p + 1])
            sent_ref[p, :share] = jnp.where(even, value[2 * p + 1], value[2 * p])
            kept_ref[p, share:] = bias
            sent_ref[p, share:] = bias

    half = jax.ShapeDtypeStruct((4 * slabs, rows, width), BF16)
    kept, sent = kernel_call(
        kernel,
        (half, half),
        "heads_weight_grads",
        20_000_000_000,
        in_specs=[smem()] + whole(6),
        out_specs=whole(2),
    )(where, *token_rows, *heads_grads, *bias_grads)
    return kept, place.sibling(sent)


def scatter_across(place, kept, arrived):
    slabs = place.slabs
    _, rows, width = kept.shape

    def kernel(kept_ref, arrived_ref, out_ref):
        for h in range(2):
            for x in range(2):
                total = kept_ref[h, 0, x].astype(F32) + arrived_ref[h, 0, x].astype(F32)
                out_ref[2 * h + x, 0] = total.astype(BF16)

    parts = kernel_call(
        kernel,
        jax.ShapeDtypeStruct((4, slabs, rows, width), BF16),
        "scatter_across",
        grid=(slabs,),
        in_specs=[pl.BlockSpec((2, 1, 2, rows, width), lambda n: (0, n, 0, 0, 0))] * 2,
        out_specs=pl.BlockSpec((4, 1, rows, width), lambda n: (0, n, 0, 0)),
    )(*(value.reshape(2, slabs, 2, rows, width) for value in (kept, arrived)))
    return parts


def scatter_slabs(parts):
    slabs, rows, width = parts.shape[1:]

    def kernel(ref, out_ref):
        out_ref[0] = sum(ref[p, 0].astype(F32) for p in range(4)).astype(BF16)

    total = kernel_call(
        kernel,
        jax.ShapeDtypeStruct((slabs, rows, width), BF16),
        "scatter_slabs",
        20_000_000_000,
        grid=(slabs,),
        in_specs=[pl.BlockSpec((4, 1, rows, width), lambda n: (0, n, 0, 0))],
        out_specs=pl.BlockSpec((1, rows, width), lambda n: (n, 0, 0)),
    )(parts)
    return total


def added(parts):
    return sum(part.astype(F32) for part in parts)


def scatter_group(place, kept, arrived, returned):
    slabs = place.slabs
    _, rows, width = kept.shape
    where = jnp.stack([place.n, place.h, place.x]).astype(jnp.int32)

    def along(where_ref, kept_ref, arrived_ref, *outs):
        for k, out in enumerate(outs):
            at = where_ref[0] ^ k
            for h in range(2):
                for x in range(2):
                    pair = kept_ref[h, at, x].astype(F32) + arrived_ref[h, at, x].astype(F32)
                    out[h, x] = pair.astype(BF16)

    parts = kernel_call(
        along,
        [jax.ShapeDtypeStruct((2, 2, rows, width), BF16)] * slabs,
        "group_along",
        in_specs=[smem()] + whole(2),
        out_specs=whole(slabs),
    )(where, *(value.reshape(2, slabs, 2, rows, width) for value in (kept, arrived)))
    parts = [parts[0]] + [place.along_slabs(parts[k], k) for k in range(1, slabs)]

    *parts, returned[0], returned[1] = lax.optimization_barrier((*parts, *returned[:2]))

    def across(where_ref, *refs):
        for (i, j), out in zip(PAIRS, refs[slabs:]):
            at = (where_ref[1] ^ i, where_ref[2] ^ j)
            out[...] = sum(ref[at].astype(F32) for ref in refs[:slabs]).astype(BF16)

    parts = kernel_call(
        across,
        [jax.ShapeDtypeStruct((rows, width), BF16)] * 4,
        "group_across",
        in_specs=[smem()] + whole(slabs),
        out_specs=whole(4),
    )(where, *parts)
    return [parts[0]] + [place.across(part, i, j) for part, (i, j) in zip(parts[1:], PAIRS[1:])]


def finish_heads(place, parts, share, scale):
    rows, width = parts[0].shape
    where = (place.h * 2 + place.x).reshape(1).astype(jnp.int32)

    def kernel(where_ref, *refs):
        sources, outs, held = refs[:4], refs[4:9], refs[9]
        for p, ref in enumerate(sources):
            held[p] = ref[...].astype(F32)
        left = left_lanes(rows)
        for which, (out, bias) in enumerate(((outs[0], outs[3]), (outs[1], None), (outs[2], outs[4]))):
            for tile in range(width // LANES):
                sides = []
                for side in range(2):
                    head = 2 * tile + side
                    value = held[(head // 3) ^ where_ref[0]]
                    t = head % 3
                    if which == 0:
                        start = t * LANES + side_of(t) * HEAD_DIM
                    else:
                        at = side_of(t) if which == 1 else 1 - side_of(t)
                        start = (3 + t) * LANES + at * HEAD_DIM
                    sides.append(half_tile(value, start, side))
                value = jnp.where(left, sides[0], sides[1])
                if which == 0:
                    value = value * scale
                lanes = slice(tile * LANES, (tile + 1) * LANES)
                out[:, lanes] = value[:share]
                if bias is not None:
                    bias[:, lanes] = value[share : share + 1]

    weight = jax.ShapeDtypeStruct((share, width), F32)
    bias = jax.ShapeDtypeStruct((1, width), F32)
    return kernel_call(
        kernel,
        (weight, weight, weight, bias, bias),
        "finish_heads",
        in_specs=[smem()] + whole(4),
        out_specs=whole(5),
        scratch_shapes=[pltpu.VMEM((4, rows, width), F32)],
    )(where, *parts)


def heads_backward(place, results, halos, ring_sum, global_at, w_heads, part):
    dqs = [results[head][0][2 * part + u] for u in range(2) for head in range(3)]
    owns = [halos[head][0] for head in range(3)]
    arrived = [halos[head][side] for head in range(3) for side in (1, 2)]
    width = w_heads.shape[0]
    rows = 512

    def kernel(at_ref, *refs):
        dq_refs, own_refs, arrived_refs = refs[:6], refs[6:9], refs[9:15]
        ring_ref, w_ref = refs[15:17]
        heads_ref, bias_ref, out_refs, held = refs[17], refs[18], refs[19:21], refs[21]
        bias = jnp.zeros((1, width), F32)
        for u in range(2):
            row = slice(u * rows, (u + 1) * rows)
            for head in range(3):
                heads_ref[row, head * LANES : (head + 1) * LANES] = dq_refs[3 * u + head][...]
                blocks = slice(u * 8, (u + 1) * 8)
                held[...] = (
                    own_refs[head][blocks]
                    + arrived_refs[2 * head][blocks].astype(F32)
                    + arrived_refs[2 * head + 1][blocks].astype(F32)
                )
                for which in range(2):
                    at = at_ref[which] - (2 * part + u) * 8

                    @pl.when((at >= 0) & (at < 8))
                    def _():
                        held[jnp.clip(at, 0, 7)] += ring_ref[which, :, head * LANES : (head + 1) * LANES]

                lanes = slice((3 + head) * LANES, (4 + head) * LANES)
                heads_ref[row, lanes] = held[...].reshape(rows, LANES).astype(BF16)
            value = heads_ref[row]
            out_refs[u][...] = dot_lanes(value, w_ref[...]).astype(BF16)
            bias = bias + jnp.sum(value.astype(F32), 0, keepdims=True)
        bias_ref[...] = bias

    own_spec = pl.BlockSpec((16, BLOCK, LANES), lambda i: (part, 0, 0))
    full = [
        pl.BlockSpec(value.shape, lambda i, rank=value.ndim: (0,) * rank)
        for value in dqs + [ring_sum, w_heads]
    ]
    shard = jax.ShapeDtypeStruct((rows, width), BF16)
    return kernel_call(
        kernel,
        (
            jax.ShapeDtypeStruct((2 * rows, width), BF16),
            jax.ShapeDtypeStruct((1, width), F32),
            shard,
            shard,
        ),
        "heads_backward",
        grid=(1,),
        in_specs=[smem()] + full[:6] + [own_spec] * 9 + full[6:],
        out_specs=[
            pl.BlockSpec((2 * rows, width), lambda i: (0, 0)),
            pl.BlockSpec((1, width), lambda i: (0, 0)),
            pl.BlockSpec((rows, width), lambda i: (0, 0)),
            pl.BlockSpec((rows, width), lambda i: (0, 0)),
        ],
        scratch_shapes=[pltpu.VMEM((8, BLOCK, LANES), F32)],
    )(global_at, *dqs, *owns, *arrived, ring_sum, w_heads)


def doc_count(position, starts_ref, count):
    total = jnp.zeros(position.shape, jnp.int32)
    for which in range(count):
        total = total + (position >= starts_ref[which]).astype(jnp.int32)
    return total


def load_slots(kv, slots_ref, base, head):
    lanes = slice(head * LANES, (head + 1) * LANES)
    return jnp.concatenate([kv[slots_ref[base + s], :, lanes] for s in range(8)], 0)


def copy_in(sources, kv, sems):
    copies = []
    start = 0
    for which, source in enumerate(sources):
        stop = start + source.shape[0]
        copies.append(pltpu.make_async_copy(source, kv.at[start:stop], sems.at[which]))
        start = stop
    for copy in copies:
        copy.start()
    for copy in copies:
        copy.wait()


def attend_forward(slots, ids, query_ids, starts, queries, pieces, part):
    heads = 3
    blocks = 32
    docs = starts.shape[0]
    many = len(pieces)

    def kernel(slots_ref, ids_ref, query_ids_ref, starts_ref, q0_ref, q1_ref, *refs):
        sources = refs[:many]
        ctx0_ref, ctx1_ref, p0_ref, p1_ref, kv, sems = refs[many:]
        step = pl.program_id(0)

        @pl.when(step == 0)
        def _():
            copy_in(sources, kv, sems)

        lane = lax.broadcasted_iota(jnp.int32, (1, LANES), 1)
        row = lax.broadcasted_iota(jnp.int32, (BLOCK, LANES), 0)
        shards = ((q0_ref, ctx0_ref, p0_ref), (q1_ref, ctx1_ref, p1_ref))
        for u, (q_ref, ctx_ref, p_ref) in enumerate(shards):
            block = part * 16 + u * 8 + step
            query_doc = doc_count(query_ids_ref[block] * BLOCK + row, starts_ref, docs)
            contexts = []
            for head in range(heads):
                base = (head * blocks + block) * 8
                slot = load_slots(kv, slots_ref, base, head)
                q = q_ref[:, head * LANES : (head + 1) * LANES]
                scores = dot_lanes(q, slot)
                tiles = []
                for tile in range(4):
                    first = ids_ref[base + 2 * tile] * BLOCK
                    second = ids_ref[base + 2 * tile + 1] * BLOCK - BLOCK
                    key_doc = doc_count(
                        jnp.where(lane < BLOCK, first + lane, second + lane), starts_ref, docs
                    )
                    tiles.append(
                        jnp.where(
                            query_doc == key_doc,
                            scores[:, tile * LANES : (tile + 1) * LANES],
                            MASKED,
                        )
                    )
                top = jnp.maximum(
                    jnp.maximum(tiles[0], tiles[1]), jnp.maximum(tiles[2], tiles[3])
                )
                top = jnp.max(top, -1, keepdims=True)
                tiles = [jnp.exp(tile - top) for tile in tiles]
                total = (tiles[0] + tiles[1]) + (tiles[2] + tiles[3])
                inverse = 1.0 / jnp.sum(total, -1, keepdims=True)
                low = jnp.concatenate([(tile * inverse).astype(BF16) for tile in tiles], 1)
                p_ref[0, head] = low
                contexts.append(matmul(low, slot))
            ctx_ref[:, :LANES] = jnp.where(lane < BLOCK, contexts[0], contexts[1]).astype(BF16)
            ctx_ref[:, LANES:] = jnp.where(lane < BLOCK, contexts[2], 0.0).astype(BF16)

    context = jax.ShapeDtypeStruct((8 * BLOCK, 2 * LANES), BF16)
    context_spec = pl.BlockSpec((BLOCK, 2 * LANES), lambda i, *_: (i, 0))
    prob = jax.ShapeDtypeStruct((8, heads, BLOCK, 8 * BLOCK), BF16)
    prob_spec = pl.BlockSpec((1, heads, BLOCK, 8 * BLOCK), lambda i, *_: (i, 0, 0, 0))
    return pl.pallas_call(
        kernel,
        out_shape=(context, context, prob, prob),
        grid_spec=pltpu.PrefetchScalarGridSpec(
            num_scalar_prefetch=4,
            grid=(8,),
            in_specs=[
                pl.BlockSpec((BLOCK, heads * LANES), lambda i, *_: (i, 0)),
                pl.BlockSpec((BLOCK, heads * LANES), lambda i, *_: (8 + i, 0)),
            ]
            + [pl.BlockSpec(memory_space=pl.ANY)] * many,
            out_specs=[context_spec, context_spec, prob_spec, prob_spec],
            scratch_shapes=[
                pltpu.VMEM((3 * blocks + 2, BLOCK, heads * LANES), BF16),
                pltpu.SemaphoreType.DMA((many,)),
            ],
        ),
        compiler_params=pltpu.CompilerParams(vmem_limit_bytes=VMEM_LIMIT),
        cost_estimate=pl.CostEstimate(
            flops=18_000_000_000, bytes_accessed=1000, transcendentals=0
        ),
        name="attend_forward",
    )(slots, ids, query_ids, starts, queries, queries, *pieces)


def attend_backward(slots, queries, probs, grads, pieces, head):
    blocks = 32
    many = len(pieces)
    lanes = slice(head * LANES, (head + 1) * LANES)

    def kernel(slots_ref, *refs):
        q_refs, p_refs, grad_refs = refs[:4], refs[4:8], refs[8:12]
        sources = refs[12 : 12 + many]
        dq_refs = refs[12 + many : 16 + many]
        own_ref, next_ref, prev_ref, glob_ref, kv, acc, sems = refs[16 + many :]
        step = pl.program_id(0)

        @pl.when(step == 0)
        def _():
            copies = []
            start = 0
            for which, source in enumerate(sources):
                stop = start + source.shape[0]
                copies.append(
                    pltpu.make_async_copy(
                        source.at[:, :, lanes], kv.at[start:stop], sems.at[which]
                    )
                )
                start = stop
            for copy in copies:
                copy.start()

            def clear(i, _):
                acc[i] = jnp.zeros(acc.shape[1:], F32)
                return _

            lax.fori_loop(0, acc.shape[0], clear, 0)
            for copy in copies:
                copy.wait()

        lane = lax.broadcasted_iota(jnp.int32, (1, LANES), 1)
        left = lane < BLOCK
        value_side = left if head % 2 == 0 else jnp.logical_not(left)
        for u in range(4):
            base = (head * blocks + u * 8 + step) * 8
            slot = jnp.concatenate([kv[slots_ref[base + s]] for s in range(8)], 0)
            grad = jnp.where(value_side, grad_refs[u][...].astype(F32), 0.0).astype(BF16)
            low = p_refs[u][0, 0]
            probs_f = low.astype(F32)
            prob_grad = dot_lanes(grad, slot)
            both = probs_f * prob_grad
            inner = jnp.sum(both, -1, keepdims=True)
            score_grad = (both - probs_f * inner).astype(BF16)
            dq = matmul(score_grad, slot)
            dq_refs[u][...] = jnp.where(value_side, 0.0, dq).astype(BF16)
            slot_grad = dot_rows(
                jnp.concatenate([score_grad, low], 0),
                jnp.concatenate([q_refs[u][...], grad], 0),
            )
            for s in range(8):
                where = slots_ref[base + s]
                acc[where] += slot_grad[s * BLOCK : (s + 1) * BLOCK]

        @pl.when(step == 7)
        def _():
            def finish(i, _):
                own_ref[i] = acc[i]
                next_ref[i] = acc[blocks + i].astype(BF16)
                prev_ref[i] = acc[2 * blocks + i].astype(BF16)
                return _

            lax.fori_loop(0, blocks, finish, 0)
            glob_ref[...] = acc[3 * blocks :]

    shape = (blocks, BLOCK, LANES)
    rows = [pl.BlockSpec((BLOCK, LANES), lambda i, *_, u=u: (8 * (u % 2) + i, head)) for u in range(4)]
    dq_spec = pl.BlockSpec((BLOCK, LANES), lambda i, *_: (i, 0))
    whole = pl.BlockSpec(shape, lambda i, *_: (0, 0, 0))
    return pl.pallas_call(
        kernel,
        out_shape=[jax.ShapeDtypeStruct((8 * BLOCK, LANES), BF16)] * 4
        + [
            jax.ShapeDtypeStruct(shape, F32),
            jax.ShapeDtypeStruct(shape, BF16),
            jax.ShapeDtypeStruct(shape, BF16),
            jax.ShapeDtypeStruct((2,) + shape[1:], F32),
        ],
        grid_spec=pltpu.PrefetchScalarGridSpec(
            num_scalar_prefetch=1,
            grid=(8,),
            in_specs=rows
            + [pl.BlockSpec((1, 1, BLOCK, 8 * BLOCK), lambda i, *_: (i, head, 0, 0))] * 4
            + [pl.BlockSpec((BLOCK, LANES), lambda i, *_: (i, head // 2))] * 4
            + [pl.BlockSpec(memory_space=pl.ANY)] * many,
            out_specs=[dq_spec] * 4
            + [whole, whole, whole, pl.BlockSpec((2,) + shape[1:], lambda i, *_: (0, 0, 0))],
            scratch_shapes=[
                pltpu.VMEM((3 * blocks + 2,) + shape[1:], BF16),
                pltpu.VMEM((3 * blocks + 2,) + shape[1:], F32),
                pltpu.SemaphoreType.DMA((many,)),
            ],
        ),
        compiler_params=pltpu.CompilerParams(vmem_limit_bytes=VMEM_LIMIT),
        cost_estimate=pl.CostEstimate(
            flops=18_000_000_000, bytes_accessed=1000, transcendentals=0
        ),
        name="attend_backward",
    )(slots, queries[0], queries[0], queries[1], queries[1], *probs, *grads, *pieces)


def norm_forward(value, gain, shift):
    center = value - jnp.mean(value, -1, keepdims=True)
    spread = jnp.mean(center * center, -1, keepdims=True)
    scale_row = lax.rsqrt(spread + NORM_EPS)
    normal = center * scale_row
    return (normal * gain + shift, normal, scale_row)


def norm_backward(grad, normal, scale_row, gain):
    gain_grad = jnp.sum(grad * normal, 0)
    shift_grad = jnp.sum(grad, 0)
    inner = grad * gain
    value_grad = scale_row * (
        inner
        - jnp.mean(inner, -1, keepdims=True)
        - normal * jnp.mean(inner * normal, -1, keepdims=True)
    )
    return (value_grad, gain_grad, shift_grad)


def local_block(place, within):
    shard = within // 8
    return (((shard % 2) ^ place.h) * 2 + ((shard // 2) ^ place.x)) * 8 + within % 8


def slot_tables(place, global_blocks, random_parts):
    ring = 2 * place.slabs
    half = 2 * place.n + place.c
    total = ring * 32
    found = []
    for arrived in random_parts:
        found.append(lax.dynamic_slice_in_dim(arrived, 3 * place.x, 3, 0).reshape(3, 2, 8, 3))
    chosen = jnp.stack(found, 2)
    chosen = jnp.where(place.h == 0, chosen, chosen[:, ::-1]).reshape(3, 32, 3)
    order = jnp.arange(32, dtype=jnp.int32)
    shard = order // 8
    query_ids = half * 32 + (((shard % 2) ^ place.x) * 2 + ((shard // 2) ^ place.h)) * 8 + order % 8
    near = (query_ids[:, None] + jnp.arange(-1, 2, dtype=jnp.int32)) % total
    ids = jnp.concatenate(
        [
            jnp.broadcast_to(near[None], (3, 32, 3)),
            jnp.broadcast_to(global_blocks, (3, 32, 2)),
            chosen,
        ],
        -1,
    )
    earlier = jnp.arange(8)[None, :] < jnp.arange(8)[:, None]
    repeated = jnp.any((ids[..., :, None] == ids[..., None, :]) & earlier, -1)
    distance = (ids // 32 - half) % ring
    region = jnp.where(distance == 0, 0, jnp.where(distance == 1, 1, 2))
    local = region * 32 + local_block(place, ids % 32)
    which = jnp.arange(8, dtype=jnp.int32)
    slots = jnp.where((which == 3) | (which == 4), 93 + which, local)
    marked = jnp.where(repeated, -1, ids)
    return (
        slots.reshape(-1).astype(jnp.int32),
        marked.reshape(-1).astype(jnp.int32),
        query_ids.astype(jnp.int32),
    )


def by_head(q, k, v):
    parts = [(m[..., :64], m[..., 64:128], m[..., 128:]) for m in (q, k, v)]
    (q0, q1, q2), (k0, k1, k2), (v0, v1, v2) = parts
    none = jnp.zeros_like(q0)
    return jnp.concatenate([none, q0, q1, none, none, q2, v0, k0, k1, v1, v2, k2], -1)


def body(
    tokens,
    cotangent,
    doc_lengths,
    global_blocks,
    random_blocks,
    query_weight,
    query_bias,
    key_weight,
    value_weight,
    value_bias,
    output_weight,
    output_bias,
    first_gain,
    first_shift,
    up_weight,
    up_bias,
    down_weight,
    down_bias,
    second_gain,
    second_shift,
):
    place = Place()
    slabs = place.slabs
    devices = 8 * slabs
    width = tokens.shape[1]
    share = query_weight.shape[0]
    hidden_width = up_weight.shape[1]
    scale = HEAD_DIM ** (-0.5)
    group = place.h * 2 + place.x
    token_group = place.h * 2 + place.c

    biases = jnp.pad(jnp.stack([query_bias, value_bias], 1), ((0, 0), (0, LANES - 2)))
    groups = pack_heads(query_weight, key_weight, value_weight, biases, scale)
    parts = [pick(groups, group)] + [
        place.across(pick(groups, group ^ (2 * i + j)), i, j) for i, j in PAIRS[1:]
    ]
    random_parts = [place.to_heads(random_blocks, 0, j) for j in range(2)]

    vectors = [
        output_bias, first_gain, first_shift, down_bias, second_gain, second_shift, up_bias
    ]
    packed = pack_rest(after(up_weight, groups), down_weight, output_weight, vectors)
    *parts, packed, random_parts[0], random_parts[1] = lax.optimization_barrier(
        (*parts, packed, *random_parts)
    )
    stacked = stack_heads(parts)
    tokens_late = after(tokens, stacked)
    token_parts = [place.to_heads(tokens_late, i, j) for i, j in PAIRS]
    heads_column = jnp.stack([stacked] + [place.along_slabs(stacked, k) for k in range(1, slabs)])
    packed = after(packed, heads_column)
    packed_column = exchange(jnp.broadcast_to(packed, (slabs,) + packed.shape), "slab")
    heads_column, *token_parts[2:] = lax.optimization_barrier((heads_column, *token_parts[2:]))
    other, *token_parts[:2] = lax.optimization_barrier((place.sibling(heads_column), *token_parts[:2]))
    arrived, bias = assemble_heads(place, heads_column, other)
    w_heads = arrived.reshape(width, width)
    bias = lax.dynamic_slice_in_dim(bias[..., :2], 2 * slabs * group, 2 * slabs).astype(F32)
    bias_query = bias[..., 0].reshape(192) * scale
    bias_value = bias[..., 1].reshape(192)
    b_heads = by_head(bias_query, jnp.zeros_like(bias_query), bias_value)

    slots, ids, query_ids = slot_tables(place, global_blocks, random_parts)
    which = jnp.arange(doc_lengths.shape[0])
    before = which[None, :] < which[:, None]
    starts = jnp.sum(jnp.where(before, doc_lengths[None, :], 0), 1).astype(jnp.int32)

    half = 2 * place.n + place.c
    token_rows = [jnp.concatenate(token_parts[2 * i : 2 * i + 2], 0) for i in range(2)]
    queries, own, following, previous = [], [], [], []

    def project(part):
        heads = (matmul(part, w_heads) + b_heads).astype(BF16)
        queries.append(heads[:, :384])
        own.append(heads[:, 384:].reshape(16, BLOCK, 384))

    def send_halo(kv):
        following.append(place.to_previous(kv))
        previous.append(place.to_next(kv))

    project(token_rows[0])
    project(token_rows[1])

    shown = []
    for i in range(2):
        at = local_block(place, global_blocks[i] % 32)
        found = jnp.where(at < 16, pick(own[0], at % 16), pick(own[1], at % 16))
        shown.append(jnp.where(global_blocks[i] // 32 == half, found, 0).astype(BF16))
    shown = jnp.stack(shown)
    shown = shown + place.sibling(shown)
    *late, shown = lax.optimization_barrier((*own, shown))
    send_halo(late[0])
    send_halo(late[1])
    mine = pick(shown, place.c)
    for k in range(1, slabs):
        mine = mine + place.along_slabs(pick(shown, place.c), k)
    theirs = place.sibling(mine)
    shared = jnp.where(place.c == 0, jnp.stack([mine, theirs]), jnp.stack([theirs, mine]))
    pieces = own + following + previous + [shared]

    packed_column = after(packed_column, mine)
    rest_column = exchange(jnp.broadcast_to(packed_column, (4,) + packed_column.shape), CHIPS)
    c2, c3, p2, p3 = attend_forward(slots, ids, query_ids, starts, queries[1], pieces, 1)
    sent = [place.to_tokens(c, i, j) for c, (i, j) in zip((c2, c3), PAIRS[2:])]
    c0, c1, p0, p1 = attend_forward(after(slots, c2), ids, query_ids, starts, queries[0], pieces, 0)
    probs = (p0, p1, p2, p3)
    mine = after(rest_column, c0)
    other = place.sibling(mine)
    sent = [place.to_tokens(c, i, j) for c, (i, j) in zip((c0, c1), PAIRS[:2])] + sent

    w_up, w_down, w_output, rest = assemble_rest(place, mine, other, share)
    w_up = w_up.reshape(width, hidden_width)
    w_down = w_down.reshape(hidden_width, width)
    vec = rest[:, :6, :share].transpose(1, 0, 2).reshape(6, width).astype(F32)
    b_output, gain_one, shift_one, b_down, gain_two, shift_two = (vec[i] for i in range(6))
    b_up = rest[:, 6, : 4 * share].reshape(hidden_width).astype(F32)

    context_tok = jnp.concatenate(sent, 1)
    w_output = w_output.reshape(4, 192, width)
    w_out = jnp.stack(
        [jnp.pad(pick(w_output, token_group ^ k), ((0, 64), (0, 0))) for k in range(4)]
    ).reshape(1024, width)

    first_sum = tokens.astype(F32) + matmul(context_tok, w_out) + b_output
    first, first_normal, first_scale = norm_forward(first_sum, gain_one, shift_one)
    first_low = first.astype(BF16)
    hidden = matmul(first_low, w_up) + b_up
    active, gelu_back = jax.vjp(partial(jax.nn.gelu, approximate=True), hidden)
    active_low = active.astype(BF16)
    second_sum = first + matmul(active_low, w_down) + b_down
    result, second_normal, second_scale = norm_forward(second_sum, gain_two, shift_two)
    second_grad, gain_two_grad, shift_two_grad = norm_backward(
        cotangent.astype(F32), second_normal, second_scale, gain_two
    )
    branch_grad = second_grad.astype(BF16)
    (hidden_grad,) = gelu_back(matmul(branch_grad, w_down.T))
    hidden_low = hidden_grad.astype(BF16)
    first_grad_in = second_grad + matmul(hidden_low, w_up.T)
    first_grad, gain_one_grad, shift_one_grad = norm_backward(
        first_grad_in, first_normal, first_scale, gain_one
    )
    attended_grad = first_grad.astype(BF16)
    context_grad = dot_lanes(attended_grad, w_out).astype(BF16)
    context_grads = [
        place.to_heads(context_grad[:, 256 * k : 256 * k + 256], i, j)
        for k, (i, j) in enumerate(PAIRS)
    ]

    down_bias_grad = jnp.sum(branch_grad.astype(F32), 0)
    up_bias_grad = jnp.sum(hidden_low.astype(F32), 0)
    output_bias_grad = jnp.sum(attended_grad.astype(F32), 0)
    vector_grads = jnp.stack(
        [output_bias_grad, gain_one_grad, shift_one_grad, down_bias_grad, gain_two_grad, shift_two_grad]
    )
    vector_grads = jnp.pad(vector_grads.reshape(6, devices, share), ((0, 2), (0, 0), (0, LANES - share)))
    wide = jnp.pad(up_bias_grad.reshape(1, devices, 4 * share), ((6, 1), (0, 0), (0, LANES - 4 * share)))
    vector_grads = (vector_grads + wide).transpose(1, 0, 2)
    kept, sent = weight_grads(
        place,
        after(active_low, context_grad),
        branch_grad,
        first_low,
        hidden_low,
        context_tok,
        attended_grad,
        vector_grads,
    )
    rest_state = (kept, place.sibling(sent))

    def head_backward(head, table):
        found = attend_backward(table, queries, probs, context_grads, pieces, head)
        return found[:4], found[4:]

    def halo(found):
        own_grad, next_grad, prev_grad, _ = found
        return own_grad, place.to_next(next_grad), place.to_previous(prev_grad)

    rest_parts = scatter_across(place, *rest_state)
    table = after(slots, rest_parts)
    rest_parts = exchange(rest_parts, CHIPS)
    results, halos = [], []
    results.append(head_backward(0, table))
    halos.append(halo(results[0][1]))
    table = after(table, results[0][1][3])
    results.append(head_backward(1, table))
    halos.append(halo(results[1][1]))

    def ring_slabs(grads):
        low = grads.astype(BF16)
        total = grads
        for k in range(1, slabs):
            total = total + place.along_slabs(low, k).astype(F32)
        return total

    ring_sum = ring_slabs(jnp.concatenate([results[0][1][3], results[1][1][3]], -1))
    table, _, *first = lax.optimization_barrier((table, results[1][1][3], *halos[0][1:]))
    halos[0] = (halos[0][0], *first)
    dqs, found = head_backward(2, table)
    ring_sum, first, second, *found = lax.optimization_barrier((ring_sum, *halos[1][1:], *found))
    halos[1] = (halos[1][0], first, second)
    results.append((dqs, found))
    halos.append(halo(found))
    rest_last = scatter_slabs(after(rest_parts, found[3]))
    ring_sum = jnp.concatenate([ring_sum, ring_slabs(results[2][1][3])], -1)
    ring_sum = ring_sum + place.sibling(ring_sum.astype(BF16)).astype(F32)
    global_at = jnp.where(
        global_blocks // 32 == half, local_block(place, global_blocks % 32), -100
    ).astype(jnp.int32)

    global_at = after(global_at, rest_last)
    rest_last = exchange(rest_last, "slab")
    heads_late, bias_late, part2, part3 = heads_backward(
        place, results, halos, ring_sum, global_at, w_heads, 1
    )
    heads_early, bias_early, part0, part1 = heads_backward(
        place, results, halos, ring_sum, after(global_at, part3), w_heads, 0
    )
    returned = [place.to_tokens(part, *pair) for part, pair in zip((part0, part1, part2, part3), PAIRS)]
    kept, arrived = heads_weight_grads(
        place, token_rows, (heads_early, heads_late), (bias_early, bias_late)
    )
    kept, arrived, returned[2], returned[3] = lax.optimization_barrier(
        (kept, arrived, returned[2], returned[3])
    )
    group_parts = scatter_group(place, kept, arrived, returned)
    tokens_grad = first_grad
    for part in returned:
        tokens_grad = tokens_grad + part.astype(F32)
    query_all, key_all, value_all, query_sum, value_sum = finish_heads(place, group_parts, share, scale)
    start = share * (place.h * 4 * slabs + 4 * place.n + 2 * place.x + place.c)
    query_bias_share = lax.dynamic_slice_in_dim(query_sum[0], start, share)
    value_bias_share = lax.dynamic_slice_in_dim(value_sum[0], start, share)
    rest_share = jnp.sum(rest_last.astype(F32), 0)
    up_share = jnp.concatenate([rest_share[i * share : (i + 1) * share] for i in range(4)], 1)
    down_share = rest_share[4 * share : 8 * share]
    output_share = rest_share[8 * share : 9 * share]
    pieces_of = [rest_share[9 * share + i, :share] for i in range(6)]

    return (
        result.astype(BF16),
        tokens_grad,
        query_all,
        query_bias_share,
        key_all,
        value_all,
        value_bias_share,
        output_share,
        pieces_of[0],
        pieces_of[1],
        pieces_of[2],
        up_share,
        rest_share[9 * share + 6, : 4 * share],
        down_share,
        pieces_of[3],
        pieces_of[4],
        pieces_of[5],
    )


def solution(mesh):
    devices = mesh.devices
    mesh = Mesh(devices.reshape(devices.shape[0], -1, 2, 2), AXES)
    rows = P(AXES, None)
    vector = P(AXES)
    tokens = P(("slab", "x", "core", "head"), None)
    return jax.shard_map(
        body,
        mesh=mesh,
        in_specs=(
            tokens,
            tokens,
            P(),
            P(),
            P("head", ("slab", "x", "core"), None),
            rows,
            vector,
            rows,
            rows,
            vector,
            rows,
            vector,
            vector,
            vector,
            rows,
            vector,
            rows,
            vector,
            vector,
            vector,
        ),
        out_specs=(
            tokens,
            tokens,
            rows,
            vector,
            rows,
            rows,
            vector,
            rows,
            vector,
            vector,
            vector,
            rows,
            vector,
            rows,
            vector,
            vector,
            vector,
        ),
        check_vma=False,
    )
```

time: 587 us -> 491 us (0.84)
  the two profiles are of different devices: /device:TPU:0 before, /device:TPU:8 now
where the time goes in v2:
time: 491 us; the launch traced here: 481 us
  Pallas kernels  163 us (33%)
  waiting for transfers between devices  122 us (25%)
  starting transfers between devices  86.4 us (18%)
  local copies, waits for them, and re-layouts  43.5 us (9%)
  matrix products  36.5 us (7%)
  other arithmetic  23 us (5%)
  between operations  7.67 us (2%)
    ppermute x56, waiting for transfers between devices, send(): return lax.ppermute(value, AXES, route)  122 us
    ppermute x56, starting transfers between devices, send(): return lax.ppermute(value, AXES, route)  63.9 us
    pallas_call x3, Pallas kernels, attend_backward(): pl.pallas_call(kernel, out_shape=[jax.ShapeDtypeStruct((8 * BLOCK, LANES)...  50.3 us
    pallas_call x2, Pallas kernels, attend_forward(): pl.pallas_call(kernel, out_shape=(context, context, prob, prob), grid_spe...  44.8 us
    dot_general x7, matrix products, matmul(): return jnp.dot(left, right, preferred_element_type=F32)  32.8 us
    all_to_all x4, starting transfers between devices, exchange(): return lax.all_to_all(value, axes, split_axis=0, concat_axis=0, tiled=True)  22.5 us
    pallas_call x1, Pallas kernels, weight_grads(): kernel_call(kernel, (half, half), 'weight_grads', 15000000000, grid_spec=...  13.1 us
    unnamed x109, local copies, waits for them, and re-layouts  12.8 us
  transfers between devices with their start and end apart: 60, of which 24 were waited for; matrix products, arithmetic and copies ran while one was open for 9% of the time, Pallas kernels for 29%

profile of v2, /device:TPU:8, one launch (start us, length us, event | category | flops | bytes accessed | tf_op | source)
XLA Modules:
  0.0 481.5 jit_solution(10160463066109498647)
XLA Ops:
  42.0 16.1 %collective-permute-done.8 = bf16[512,768]{1,0:T(8,128)(2,1)S(1)} collective-permute-done((bf16[512,768]{1,0:T(8,128)(2,1)}, bf16[512,768]{1,0:T(8,128)(2,1)S(1)}, u32[]{:S(2)}, u32[]{:S(2)}) %collective-permute-start.8) | collective-permute-done | bytes 786464 | tf_op jit(solution)/shard_map/ppermute | solution.py:53
  93.2 13.0 %collective-permute-done.19 = bf16[64,384]{1,0:T(8,128)(2,1)S(1)} collective-permute-done((bf16[64,384]{1,0:T(8,128)(2,1)S(1)}, bf16[64,384]{1,0:T(8,128)(2,1)S(1)}, u32[]{:S(2)}, u32[]{:S(2)}) %collective-permute-start.19) | collective-permute-done | bytes 49184 | tf_op jit(solution)/shard_map/ppermute | solution.py:53
  120.3 14.0 %collective-permute-done.15.refs_3_.refs_15_ = bf16[16,64,384]{2,1,0:T(8,128)(2,1)} collective-permute-done((bf16[16,64,384]{2,1,0:T(8,128)(2,1)}, bf16[16,64,384]{2,1,0:T(8,128)(2,1)}, u32[]{:S(2)}, u32[]{:S(2)}) %collective-permute-start.15) | collective-permute-done | bytes 786464 | tf_op jit(solution)/shard_map/ppermute | solution.py:53
  134.2 22.3 %attend_forward.2 = (bf16[512,256]{1,0:T(8,128)(2,1)}, bf16[512,256]{1,0:T(8,128)(2,1)}, bf16[8,3,64,512]{3,2,1,0:T(8,128)(2,1)}, bf16[8,3,64,512]{3,2,1,0:T(8,128)(2,1)}) custom-call(s32[768]{0:T(1024)} %get-tuple-element.175.slots_ref, s32[768]{0:T(1024)} %get-tuple-element.290.ids_ref, s32[32]{0:T(128)} %copy-done.38, s32[8]{0:T(128)} %select_reduce_fusion.starts_ref, ...), custom_call_target="tpu_custom_call" | custom-call | flops 17999998976 | bytes 1000 | tf_op jit(solution)/shard_map/attend_forward/pallas_call | solution.py:628
  156.6 22.4 %attend_forward.3 = (bf16[512,256]{1,0:T(8,128)(2,1)}, bf16[512,256]{1,0:T(8,128)(2,1)}, bf16[8,3,64,512]{3,2,1,0:T(8,128)(2,1)}, bf16[8,3,64,512]{3,2,1,0:T(8,128)(2,1)}) custom-call(s32[768]{0:T(1024)} %get-tuple-element.175.slots_ref, s32[768]{0:T(1024)} %get-tuple-element.290.ids_ref, s32[32]{0:T(128)} %copy-done.38, s32[8]{0:T(128)} %select_reduce_fusion.starts_ref, ...), custom_call_target="tpu_custom_call" | custom-call | flops 17999998976 | bytes 1000 | tf_op jit(solution)/shard_map/attend_forward/pallas_call | solution.py:628
  193.1 6.5 %collective-permute-done.25 = bf16[512,256]{1,0:T(8,128)(2,1)S(1)} collective-permute-done((bf16[512,256]{1,0:T(8,128)(2,1)S(1)}, bf16[512,256]{1,0:T(8,128)(2,1)S(1)}, u32[]{:S(2)}, u32[]{:S(2)}) %collective-permute-start.25) | collective-permute-done | bytes 262176 | tf_op jit(solution)/shard_map/ppermute | solution.py:53
  200.5 8.4 %assemble_rest.1 = (bf16[2,4,2,2,24,3072]{5,4,3,2,1,0:T(8,128)(2,1)}, bf16[2,4,2,2,96,768]{5,4,3,2,1,0:T(8,128)(2,1)}, bf16[2,4,2,2,24,768]{5,4,3,2,1,0:T(8,128)(2,1)}, bf16[2,4,2,2,8,768]{5,4,3,2,1,0:T(8,128)(2,1)}) custom-call(s32[1]{0:T(128)} %bitcast.20.where_ref, bf16[4,4,224,768]{3,2,1,0:T(8,128)(2,1)} %all-to-all-done.1.mine_ref, ...), custom_call_target="tpu_custom_call" | custom-call | flops 1000 | bytes 1000 | tf_op jit(solution)/shard_map/assemble_rest/pallas_call | solution.py:260
  217.6 8.2 %multiply_convert_fusion = (bf16[512,3072]{1,0:T(8,128)(2,1)S(1)}, f32[512,3072]{1,0:T(8,128)}) fusion(f32[3072]{0:T(1024)S(1)} %reshape.288, bf16[512,768]{1,0:T(8,128)(2,1)S(1)} %fusion.14, bf16[768,3072]{1,0:T(8,128)(2,1)} %bitcast.170), kind=kOutput, calls=%fused_computation.10 | convolution fusion | flops 2431647744 | bytes 14954496 | tf_op jit(solution)/shard_map/dot_general | solution.py:25
  225.8 6.2 %fusion.56 = (f32[512]{0:T(512)S(1)}, f32[512,768]{1,0:T(8,128)S(1)}) fusion(f32[768]{0:T(1024)S(1)} %add.506, bf16[512,3072]{1,0:T(8,128)(2,1)S(1)} %get-tuple-element.160.active_ref, bf16[3072,768]{1,0:T(8,128)(2,1)} %bitcast.174, f32[768]{0:T(1024)S(1)} %add.498, f32[768]{0:T(1024)S(1)} %mul.246, f32[512]{0:T(512)S(1)} %add_rsqrt_fusion.1, ...), kind=kOutput, calls=%fused_computation.213 | convolution fusion | flops 2418671104 | bytes 11025408 | tf_op jit(solution)/shard_map/dot_general | solution.py:25
  237.2 9.7 %convert_reduce_fusion = (f32[3072]{0:T(1024)S(1)}, bf16[512,3072]{1,0:T(8,128)(2,1)S(1)}) fusion(f32[512,3072]{1,0:T(8,128)} %get-tuple-element.297, f32[3072]{0:T(1024)S(1)} %reshape.288, bf16[512,768]{1,0:T(8,128)(2,1)S(1)} %get-tuple-element.248.branch_ref, bf16[3072,768]{1,0:T(8,128)(2,1)} %bitcast.175), kind=kOutput, calls=%fused_computation.9 | convolution fusion | flops 2452091904 | bytes 14966784 | tf_op jit(solution)/shard_map/dot_general | solution.py:25
  258.3 13.1 %weight_grads.1 = (bf16[16,224,768]{2,1,0:T(8,128)(2,1)}, bf16[16,224,768]{2,1,0:T(8,128)(2,1)}) custom-call(s32[2]{0:T(128)} %pad_add_fusion.4.where_ref, bf16[512,3072]{1,0:T(8,128)(2,1)} %copy-done.48, bf16[512,768]{1,0:T(8,128)(2,1)} %copy-done.19, bf16[512,1024]{1,0:T(8,128)(2,1)} %copy.81.first_ref, bf16[512,3072]{1,0:T(8,128)(2,1)} %copy-done.47, ...), custom_call_target="tpu_custom_call" | custom-call | flops 15000000512 | bytes 1000 | tf_op jit(solution)/shard_map/weight_grads/pallas_call | solution.py:306
  280.8 7.2 %scatter_across.1 = bf16[4,4,224,768]{3,2,1,0:T(8,128)(2,1)} custom-call(bf16[2,4,2,224,768]{4,3,2,1,0:T(8,128)(2,1)} %bitcast.128, bf16[2,4,2,224,768]{4,3,2,1,0:T(8,128)(2,1)} %bitcast.55.arrived_ref), custom_call_target="tpu_custom_call" | custom-call | flops 1000 | bytes 1000 | tf_op jit(solution)/shard_map/scatter_across/pallas_call | solution.py:368
  294.0 16.8 %attend_backward.3 = (bf16[512,128]{1,0:T(8,128)(2,1)}, bf16[512,128]{1,0:T(8,128)(2,1)}, bf16[512,128]{1,0:T(8,128)(2,1)}, bf16[512,128]{1,0:T(8,128)(2,1)}, f3...) custom-call(s32[768]{0:T(1024)} %get-tuple-element.175.slots_ref, ...), custom_call_target="tpu_custom_call" | custom-call | flops 17999998976 | bytes 1000 | tf_op jit(solution)/shard_map/attend_backward/pallas_call | solution.py:726
  312.5 16.8 %attend_backward.4 = (bf16[512,128]{1,0:T(8,128)(2,1)}, bf16[512,128]{1,0:T(8,128)(2,1)}, bf16[512,128]{1,0:T(8,128)(2,1)}, bf16[512,128]{1,0:T(8,128)(2,1)}, f3...) custom-call(s32[768]{0:T(1024)} %get-tuple-element.175.slots_ref, ...), custom_call_target="tpu_custom_call" | custom-call | flops 17999998976 | bytes 1000 | tf_op jit(solution)/shard_map/attend_backward/pallas_call | solution.py:726
  339.3 16.8 %attend_backward.5 = (bf16[512,128]{1,0:T(8,128)(2,1)}, bf16[512,128]{1,0:T(8,128)(2,1)}, bf16[512,128]{1,0:T(8,128)(2,1)}, bf16[512,128]{1,0:T(8,128)(2,1)}, f3...) custom-call(s32[768]{0:T(1024)} %get-tuple-element.175.slots_ref, ...), custom_call_target="tpu_custom_call" | custom-call | flops 17999998976 | bytes 1000 | tf_op jit(solution)/shard_map/attend_backward/pallas_call | solution.py:726
  375.0 7.0 %all-to-all-start.3 = ((bf16[4,224,768]{2,1,0:T(8,128)(2,1)}), bf16[4,224,768]{2,1,0:T(8,128)(2,1)S(1)}, u32[]{:S(2)}, u32[]{:S(2)}) async-start(bf16[4,224,768]{2,1,0:T(8,128)(2,1)} %scatter_slabs.1), calls=%async_computation.3 | async-start | bytes 2752512 | tf_op jit(solution)/shard_map/all_to_all | solution.py:84
  382.7 6.2 %heads_backward.2 = (bf16[1024,768]{1,0:T(8,128)(2,1)}, f32[1,768]{1,0:T(1,128)}, bf16[512,768]{1,0:T(8,128)(2,1)}, bf16[512,768]{1,0:T(8,128)(2,1)}) custom-call(s32[2]{0:T(128)} %compare_select_fusion.at_ref, bf16[512,128]{1,0:T(8,128)(2,1)} %get-tuple-element.183.refs_0_, bf16[512,128]{1,0:T(8,128)(2,1)} %get-tuple-element.184.refs_1_, ...), custom_call_target="tpu_custom_call" | custom-call | flops 1000 | bytes 1000 | tf_op jit(solution)/shard_map/heads_backward/pallas_call | solution.py:524
  389.0 6.2 %heads_backward.3 = (bf16[1024,768]{1,0:T(8,128)(2,1)}, f32[1,768]{1,0:T(1,128)}, bf16[512,768]{1,0:T(8,128)(2,1)}, bf16[512,768]{1,0:T(8,128)(2,1)}) custom-call(s32[2]{0:T(128)} %compare_select_fusion.at_ref, bf16[512,128]{1,0:T(8,128)(2,1)} %get-tuple-element.201.refs_0_, bf16[512,128]{1,0:T(8,128)(2,1)} %get-tuple-element.202.refs_1_, ...), custom_call_target="tpu_custom_call" | custom-call | flops 1000 | bytes 1000 | tf_op jit(solution)/shard_map/heads_backward/pallas_call | solution.py:524
  395.2 6.7 %heads_weight_grads.1 = (bf16[16,32,768]{2,1,0:T(8,128)(2,1)}, bf16[16,32,768]{2,1,0:T(8,128)(2,1)}) custom-call(s32[1]{0:T(128)} %bitcast.20.where_ref, bf16[1024,768]{1,0:T(8,128)(2,1)} %copy-done.21, bf16[1024,768]{1,0:T(8,128)(2,1)} %copy-done.22, bf16[1024,768]{1,0:T(8,128)(2,1)} %get-tuple-element.207.g0_ref, ...), custom_call_target="tpu_custom_call" | custom-call | flops 20000000000 | bytes 1000 | tf_op jit(solution)/shard_map/heads_weight_grads/pallas_call | solution.py:347
  405.0 7.5 %collective-permute-start.51 = (bf16[512,768]{1,0:T(8,128)(2,1)}, bf16[512,768]{1,0:T(8,128)(2,1)}, u32[]{:S(2)}, u32[]{:S(2)}) collective-permute-start(bf16[512,768]{1,0:T(8,128)(2,1)} %get-tuple-element.220), channel_id=1, source_target_pairs={{0,0},{1,2},{2,1},{3,3},{4,4},{5,6},{6,5},{7,7},{8,8},{9,10},{10,9... | collective-permute-start | bytes 2359304 | tf_op jit(solution)/shard_map/ppermute | solution.py:53
  413.0 18.0 %collective-permute-done.46 = bf16[512,768]{1,0:T(8,128)(2,1)} collective-permute-done((bf16[512,768]{1,0:T(8,128)(2,1)}, bf16[512,768]{1,0:T(8,128)(2,1)}, u32[]{:S(2)}, u32[]{:S(2)}) %collective-permute-start.46) | collective-permute-done | bytes 786464 | tf_op jit(solution)/shard_map/ppermute | solution.py:53
  431.0 7.9 %collective-permute-done.47 = bf16[512,768]{1,0:T(8,128)(2,1)} collective-permute-done((bf16[512,768]{1,0:T(8,128)(2,1)}, bf16[512,768]{1,0:T(8,128)(2,1)}, u32[]{:S(2)}, u32[]{:S(2)}) %collective-permute-start.47) | collective-permute-done | bytes 786464 | tf_op jit(solution)/shard_map/ppermute | solution.py:53
  445.0 7.2 %collective-permute-done.48.refs_1_ = bf16[2,2,32,768]{3,2,1,0:T(8,128)(2,1)S(1)} collective-permute-done((bf16[2,2,32,768]{3,2,1,0:T(8,128)(2,1)}, bf16[2,2,32,768]{3,2,1,0:T(8,128)(2,1)S(1)}, u32[]{:S(2)}, u32[]{:S(2)}) %collective-permute-start.48) | collective-permute-done | bytes 196640 | tf_op jit(solution)/shard_map/ppermute | solution.py:53
  452.3 6.0 %collective-permute-done.49.refs_2_ = bf16[2,2,32,768]{3,2,1,0:T(8,128)(2,1)S(1)} collective-permute-done((bf16[2,2,32,768]{3,2,1,0:T(8,128)(2,1)}, bf16[2,2,32,768]{3,2,1,0:T(8,128)(2,1)S(1)}, u32[]{:S(2)}, u32[]{:S(2)}) %collective-permute-start.49) | collective-permute-done | bytes 196640 | tf_op jit(solution)/shard_map/ppermute | solution.py:53
  (360 shorter events, 203.9 us)
Async XLA Ops:
  20.8 37.2 %collective-permute-start.8 = (bf16[512,768]{1,0:T(8,128)(2,1)}, bf16[512,768]{1,0:T(8,128)(2,1)S(1)}, u32[]{:S(2)}, u32[]{:S(2)}) collective-permute-start(bf16[512,768]{1,0:T(8,128)(2,1)} %param.20), channel_id=1, source_target_pairs={{0,16},{1,18},{2,17},{3,19},{4,20},{5,22},{6,21},{7,23},{8,24},{9,... | collective-permute-start | bytes 2359304 | tf_op jit(solution)/shard_map/ppermute | solution.py:53
  22.3 35.9 %collective-permute-start.9 = (bf16[512,768]{1,0:T(8,128)(2,1)}, bf16[512,768]{1,0:T(8,128)(2,1)}, u32[]{:S(2)}, u32[]{:S(2)}) collective-permute-start(bf16[512,768]{1,0:T(8,128)(2,1)} %param.20), channel_id=1, source_target_pairs={{0,18},{1,16},{2,19},{3,17},{4,22},{5,20},{6,23},{7,21},{8,26},{9,... | collective-permute-start | bytes 2359304 | tf_op jit(solution)/shard_map/ppermute | solution.py:53
  28.7 40.8 %collective-permute-start.11 = (bf16[512,768]{1,0:T(8,128)(2,1)}, bf16[512,768]{1,0:T(8,128)(2,1)S(1)}, u32[]{:S(2)}, u32[]{:S(2)}) collective-permute-start(bf16[512,768]{1,0:T(8,128)(2,1)} %param.20), channel_id=1, source_target_pairs={{0,0},{1,2},{2,1},{3,3},{4,4},{5,6},{6,5},{7,7},{8,8},{9,10},{10,9... | collective-permute-start | bytes 2359304 | tf_op jit(solution)/shard_map/ppermute | solution.py:53
  35.1 34.4 %collective-permute-start.12 = (bf16[512,768]{1,0:T(8,128)(2,1)}, bf16[512,768]{1,0:T(8,128)(2,1)S(1)}, u32[]{:S(2)}, u32[]{:S(2)}) collective-permute-start(bf16[512,768]{1,0:T(8,128)(2,1)} %param.20), channel_id=1, source_target_pairs={{0,2},{1,0},{2,3},{3,1},{4,6},{5,4},{6,7},{7,5},{8,10},{9,8},{10,1... | collective-permute-start | bytes 2359304 | tf_op jit(solution)/shard_map/ppermute | solution.py:53
  61.8 46.6 %all-to-all-start = ((bf16[4,224,768]{2,1,0:T(8,128)(2,1)}), bf16[4,224,768]{2,1,0:T(8,128)(2,1)S(1)}, u32[]{:S(2)}, u32[]{:S(2)}) async-start(bf16[4,224,768]{2,1,0:T(8,128)(2,1)} %broadcast_in_dim.117), calls=%async_computation | async-start | bytes 2752512 | tf_op jit(solution)/shard_map/all_to_all | solution.py:84
  91.2 29.1 %collective-permute-start.14 = (bf16[16,64,384]{2,1,0:T(8,128)(2,1)S(1)}, bf16[16,64,384]{2,1,0:T(8,128)(2,1)S(1)}, u32[]{:S(2)}, u32[]{:S(2)}) collective-permute-start(bf16[16,64,384]{2,1,0:T(8,128)(2,1)S(1)} %bitcast.147), channel_id=1, source_target_pairs={{0,13},{1,0},{2,15},{3,2},{4,1},{5,4},{6,3},{7,6},{8,5},{9,8},{10,... | collective-permute-start | bytes 2359304 | tf_op jit(solution)/shard_map/ppermute | solution.py:53
  91.4 42.8 %collective-permute-start.16 = (bf16[16,64,384]{2,1,0:T(8,128)(2,1)S(1)}, bf16[16,64,384]{2,1,0:T(8,128)(2,1)}, u32[]{:S(2)}, u32[]{:S(2)}) collective-permute-start(bf16[16,64,384]{2,1,0:T(8,128)(2,1)S(1)} %bitcast.148), channel_id=1, source_target_pairs={{0,1},{1,4},{2,3},{3,6},{4,5},{5,8},{6,7},{7,10},{8,9},{9,12},{10,... | collective-permute-start | bytes 2359304 | tf_op jit(solution)/shard_map/ppermute | solution.py:53
  91.8 42.4 %collective-permute-start.15 = (bf16[16,64,384]{2,1,0:T(8,128)(2,1)}, bf16[16,64,384]{2,1,0:T(8,128)(2,1)}, u32[]{:S(2)}, u32[]{:S(2)}) collective-permute-start(bf16[16,64,384]{2,1,0:T(8,128)(2,1)} %bitcast.139), channel_id=1, source_target_pairs={{0,13},{1,0},{2,15},{3,2},{4,1},{5,4},{6,3},{7,6},{8,5},{9,8},{10,... | collective-permute-start | bytes 2359304 | tf_op jit(solution)/shard_map/ppermute | solution.py:53
  106.2 28.0 %collective-permute-start.17 = (bf16[16,64,384]{2,1,0:T(8,128)(2,1)}, bf16[16,64,384]{2,1,0:T(8,128)(2,1)}, u32[]{:S(2)}, u32[]{:S(2)}) collective-permute-start(bf16[16,64,384]{2,1,0:T(8,128)(2,1)} %bitcast.140), channel_id=1, source_target_pairs={{0,1},{1,4},{2,3},{3,6},{4,5},{5,8},{6,7},{7,10},{8,9},{9,12},{10,... | collective-permute-start | bytes 2359304 | tf_op jit(solution)/shard_map/ppermute | solution.py:53
  111.3 67.8 %all-to-all-start.1 = ((bf16[4,4,224,768]{3,2,1,0:T(8,128)(2,1)}), bf16[4,4,224,768]{3,2,1,0:T(8,128)(2,1)}, u32[]{:S(2)}, u32[]{:S(2)}) async-start(bf16[4,4,224,768]{3,2,1,0:T(8,128)(2,1)} %broadcast_in_dim.118), calls=%async_computation.1 | async-start | bytes 11010048 | tf_op jit(solution)/shard_map/all_to_all | solution.py:84
  179.1 21.5 %collective-permute-start.26 = (bf16[4,4,224,768]{3,2,1,0:T(8,128)(2,1)}, bf16[4,4,224,768]{3,2,1,0:T(8,128)(2,1)}, u32[]{:S(2)}, u32[]{:S(2)}) collective-permute-start(bf16[4,4,224,768]{3,2,1,0:T(8,128)(2,1)} %all-to-all-done.1.mine_ref), channel_id=1, source_target_pairs={{0,1},{1,0},{2,3},{3,2},{4,5},{5,4},{6,7},{7,6},{8,9},{9,8},{10,11... | collective-permute-start | bytes 16515080 | tf_op jit(solution)/shard_map/ppermute | solution.py:53
  272.2 20.9 %collective-permute-start.28 = (bf16[512,256]{1,0:T(8,128)(2,1)}, bf16[512,256]{1,0:T(8,128)(2,1)S(1)}, u32[]{:S(2)}, u32[]{:S(2)}) collective-permute-start(bf16[512,256]{1,0:T(8,128)(2,1)} %get-tuple-element.268), channel_id=1, source_target_pairs={{0,0},{1,2},{2,1},{3,3},{4,4},{5,6},{6,5},{7,7},{8,8},{9,10},{10,9... | collective-permute-start | bytes 786440 | tf_op jit(solution)/shard_map/ppermute | solution.py:53
  273.8 19.3 %collective-permute-start.29 = (bf16[512,256]{1,0:T(8,128)(2,1)S(1)}, bf16[512,256]{1,0:T(8,128)(2,1)S(1)}, u32[]{:S(2)}, u32[]{:S(2)}) collective-permute-start(bf16[512,256]{1,0:T(8,128)(2,1)S(1)} %get-tuple-element.267), channel_id=1, source_target_pairs={{0,2},{1,0},{2,3},{3,1},{4,6},{5,4},{6,7},{7,5},{8,10},{9,8},{10,1... | collective-permute-start | bytes 786440 | tf_op jit(solution)/shard_map/ppermute | solution.py:53
  288.0 82.2 %all-to-all-start.2 = ((bf16[4,4,224,768]{3,2,1,0:T(8,128)(2,1)}), bf16[4,4,224,768]{3,2,1,0:T(8,128)(2,1)}, u32[]{:S(2)}, u32[]{:S(2)}) async-start(bf16[4,4,224,768]{3,2,1,0:T(8,128)(2,1)} %scatter_across.1), calls=%async_computation.2 | async-start | bytes 11010048 | tf_op jit(solution)/shard_map/all_to_all | solution.py:84
  310.7 28.5 %collective-permute-start.37 = (bf16[32,64,128]{2,1,0:T(8,128)(2,1)}, bf16[32,64,128]{2,1,0:T(8,128)(2,1)S(1)}, u32[]{:S(2)}, u32[]{:S(2)}) collective-permute-start(bf16[32,64,128]{2,1,0:T(8,128)(2,1)} %get-tuple-element.173), channel_id=1, source_target_pairs={{0,1},{1,4},{2,3},{3,6},{4,5},{5,8},{6,7},{7,10},{8,9},{9,12},{10,... | collective-permute-start | bytes 1572872 | tf_op jit(solution)/shard_map/ppermute | solution.py:53
  310.9 28.3 %collective-permute-start.38 = (bf16[32,64,128]{2,1,0:T(8,128)(2,1)}, bf16[32,64,128]{2,1,0:T(8,128)(2,1)S(1)}, u32[]{:S(2)}, u32[]{:S(2)}) collective-permute-start(bf16[32,64,128]{2,1,0:T(8,128)(2,1)} %get-tuple-element.174), channel_id=1, source_target_pairs={{0,13},{1,0},{2,15},{3,2},{4,1},{5,4},{6,3},{7,6},{8,5},{9,8},{10,... | collective-permute-start | bytes 1572872 | tf_op jit(solution)/shard_map/ppermute | solution.py:53
  334.5 21.6 %collective-permute-start.35 = (bf16[32,64,128]{2,1,0:T(8,128)(2,1)}, bf16[32,64,128]{2,1,0:T(8,128)(2,1)S(1)}, u32[]{:S(2)}, u32[]{:S(2)}) collective-permute-start(bf16[32,64,128]{2,1,0:T(8,128)(2,1)} %get-tuple-element.171), channel_id=1, source_target_pairs={{0,1},{1,4},{2,3},{3,6},{4,5},{5,8},{6,7},{7,10},{8,9},{9,12},{10,... | collective-permute-start | bytes 1572872 | tf_op jit(solution)/shard_map/ppermute | solution.py:53
  336.9 19.2 %collective-permute-start.36 = (bf16[32,64,128]{2,1,0:T(8,128)(2,1)}, bf16[32,64,128]{2,1,0:T(8,128)(2,1)S(1)}, u32[]{:S(2)}, u32[]{:S(2)}) collective-permute-start(bf16[32,64,128]{2,1,0:T(8,128)(2,1)} %get-tuple-element.172), channel_id=1, source_target_pairs={{0,13},{1,0},{2,15},{3,2},{4,1},{5,4},{6,3},{7,6},{8,5},{9,8},{10,... | collective-permute-start | bytes 1572872 | tf_op jit(solution)/shard_map/ppermute | solution.py:53
  375.0 102.7 %all-to-all-start.3 = ((bf16[4,224,768]{2,1,0:T(8,128)(2,1)}), bf16[4,224,768]{2,1,0:T(8,128)(2,1)S(1)}, u32[]{:S(2)}, u32[]{:S(2)}) async-start(bf16[4,224,768]{2,1,0:T(8,128)(2,1)} %scatter_slabs.1), calls=%async_computation.3 | async-start | bytes 2752512 | tf_op jit(solution)/shard_map/all_to_all | solution.py:84
  401.8 29.2 %collective-permute-start.46 = (bf16[512,768]{1,0:T(8,128)(2,1)}, bf16[512,768]{1,0:T(8,128)(2,1)}, u32[]{:S(2)}, u32[]{:S(2)}) collective-permute-start(bf16[512,768]{1,0:T(8,128)(2,1)} %get-tuple-element.213), channel_id=1, source_target_pairs={{0,16},{1,18},{2,17},{3,19},{4,20},{5,22},{6,21},{7,23},{8,24},{9,... | collective-permute-start | bytes 2359304 | tf_op jit(solution)/shard_map/ppermute | solution.py:53
  403.8 35.1 %collective-permute-start.47 = (bf16[512,768]{1,0:T(8,128)(2,1)}, bf16[512,768]{1,0:T(8,128)(2,1)}, u32[]{:S(2)}, u32[]{:S(2)}) collective-permute-start(bf16[512,768]{1,0:T(8,128)(2,1)} %get-tuple-element.199), channel_id=1, source_target_pairs={{0,17},{1,19},{2,16},{3,18},{4,21},{5,23},{6,20},{7,22},{8,25},{9,... | collective-permute-start | bytes 2359304 | tf_op jit(solution)/shard_map/ppermute | solution.py:53
  405.0 40.0 %collective-permute-start.51 = (bf16[512,768]{1,0:T(8,128)(2,1)}, bf16[512,768]{1,0:T(8,128)(2,1)}, u32[]{:S(2)}, u32[]{:S(2)}) collective-permute-start(bf16[512,768]{1,0:T(8,128)(2,1)} %get-tuple-element.220), channel_id=1, source_target_pairs={{0,0},{1,2},{2,1},{3,3},{4,4},{5,6},{6,5},{7,7},{8,8},{9,10},{10,9... | collective-permute-start | bytes 2359304 | tf_op jit(solution)/shard_map/ppermute | solution.py:53
  412.4 32.6 %collective-permute-start.52 = (bf16[512,768]{1,0:T(8,128)(2,1)}, bf16[512,768]{1,0:T(8,128)(2,1)}, u32[]{:S(2)}, u32[]{:S(2)}) collective-permute-start(bf16[512,768]{1,0:T(8,128)(2,1)} %get-tuple-element.221), channel_id=1, source_target_pairs={{0,1},{1,3},{2,0},{3,2},{4,5},{5,7},{6,4},{7,6},{8,9},{9,11},{10,8... | collective-permute-start | bytes 2359304 | tf_op jit(solution)/shard_map/ppermute | solution.py:53
  444.2 19.1 %collective-permute-start.50 = (bf16[2,2,32,768]{3,2,1,0:T(8,128)(2,1)}, bf16[2,2,32,768]{3,2,1,0:T(8,128)(2,1)S(1)}, u32[]{:S(2)}, u32[]{:S(2)}) collective-permute-start(bf16[2,2,32,768]{3,2,1,0:T(8,128)(2,1)} %get-tuple-element.219), channel_id=1, source_target_pairs={{0,12},{1,13},{2,14},{3,15},{4,8},{5,9},{6,10},{7,11},{8,4},{9,5},... | collective-permute-start | bytes 589832 | tf_op jit(solution)/shard_map/ppermute | solution.py:53
  (87 other events, 933.3 us)
